TPU v7x, 256 devices: a whole 4x4x8 slice. The times are simulated.
256 devices in a mesh: section: 4 (over x), dp: 8 (over z_hi, core), tensor: 8 (over y, z_lo).
Axes of the slice: x: 4, y: 4, z: 8 (z_hi: 4, z_lo: 2; z = z_hi * 2 + z_lo), core: 2. Of those that a mesh axis runs over, the one named last changes fastest.
Arguments:
- features: bfloat16 [6144, 8192], P(('dp', 'section'), 'tensor'), parts along dimension 0, may hold values from -6 to 6
- key_weight: bfloat16 [4, 8192, 1024], P('section', 'tensor'), may hold values from -0.0625 to 0.0625
- value_weight: bfloat16 [4, 8192, 1024], P('section', 'tensor'), may hold values from -0.0625 to 0.0625
- queries: bfloat16 [4, 2048, 8192], P('section', 'dp', 'tensor'), parts along dimension 1, may hold values from -60 to 60
- out_grad: bfloat16 [4, 2048, 8192], P('section', 'dp', 'tensor'), parts along dimension 1, may hold values from -6 to 6
- tile_count: int32 [32], P('dp'), parts along dimension 0, may hold values from 96 to 192, as said below
- tile_last: int32 [2048], P('dp'), parts along dimension 0, may hold values from 0 to 3, as said below
Outputs:
- attended: bfloat16 [4, 2048, 8192], P('section', 'dp', 'tensor'), parts along dimension 1
- feature_grad: bfloat16 [6144, 8192], P(('dp', 'section'), 'tensor'), parts along dimension 0
- key_weight_grad: bfloat16 [4, 8192, 8192], P('section', 'tensor', 'dp'), parts along dimension 2
- value_weight_grad: bfloat16 [4, 8192, 8192], P('section', 'tensor', 'dp'), parts along dimension 2
There are 8 independent parts, one for each index of `dp`. A program takes and returns all parts, laid end to end along the dimension named above; an argument that names none is the same for every part. Nothing has to cross between parts.
Inputs may be any that keep to these rules, and one draw needn't show every extreme that they name: `tile_count`: each tile has between 96 and 192 image tokens; some tile is full. `tile_last`: every text token sees tile 0; some token sees every tile.
All inputs are finite; a program needn't handle non-finite values.
Results may differ from a plain program's by a relative error of at most 0.015.
The roundings to bfloat16 on the way count: a program that leaves them out, or rounds other values in their place, can miss the bound.
Values may be sent and summed in bfloat16 or wider, within the bound.
A program may use at most 128 MiB of HBM per device.

v0:
```python
import jax
import jax.numpy as jnp
from jax import lax
from jax.sharding import PartitionSpec as P

HQ = 64
KVH = 8
HD = 128


def per_device(features, key_weight, value_weight, queries, out_grad, tile_count, tile_last):
    sections = lax.axis_size("section")
    tile = features.shape[0]
    img = tile * sections
    key_w = key_weight[0]
    value_w = value_weight[0]
    query = queries[0]
    dout = out_grad[0]
    seq = query.shape[0]
    group = HQ // KVH
    scale = HD ** (-0.5)
    gathered = lax.all_gather(features, "section", axis=0, tiled=True)
    partial_sums = jnp.stack(
        [
            jnp.dot(gathered, key_w, preferred_element_type=jnp.float32),
            jnp.dot(gathered, value_w, preferred_element_type=jnp.float32),
        ],
        axis=1,
    )
    key_val = lax.psum_scatter(partial_sums, "tensor", scatter_dimension=2, tiled=True).astype(
        jnp.bfloat16
    )
    local_width = key_val.shape[2]
    kv_local = local_width // HD
    keys = key_val[:, 0, :].reshape(img, kv_local, HD)
    values = key_val[:, 1, :].reshape(img, kv_local, HD)
    slots = jnp.arange(img, dtype=jnp.int32)
    tile_of = slots // tile
    slot_in = slots % tile
    owner = (tile_of[:, None] == jnp.arange(sections, dtype=jnp.int32)[None, :]).astype(jnp.int32)
    count_of = jnp.sum(owner * tile_count[None, :], axis=1)
    present = slot_in < count_of
    visible = (present[None, :] & (tile_of[None, :] <= tile_last[:, None])).astype(jnp.int32)
    q_heads = query.reshape(seq, kv_local, group, HD)
    scores = jnp.einsum("skgd,jkd->kgsj", q_heads, keys, preferred_element_type=jnp.float32) * scale
    masked = jnp.where(visible[None, None] > 0, scores, -jnp.inf)
    top = jnp.max(masked, axis=-1, keepdims=True)
    expo = jnp.exp(masked - top)
    probs = expo / jnp.sum(expo, axis=-1, keepdims=True)
    probs16 = probs.astype(jnp.bfloat16)
    out = jnp.einsum("kgsj,jkd->skgd", probs16, values, preferred_element_type=jnp.float32)
    out = out.reshape(seq, kv_local * group * HD).astype(jnp.bfloat16)
    g_heads = dout.reshape(seq, kv_local, group, HD)
    dprobs = jnp.einsum("skgd,jkd->kgsj", g_heads, values, preferred_element_type=jnp.float32)
    delta = jnp.sum(probs * dprobs, axis=-1, keepdims=True)
    dscores = (probs * (dprobs - delta) * scale).astype(jnp.bfloat16)
    dkeys = jnp.einsum("kgsj,skgd->jkd", dscores, q_heads, preferred_element_type=jnp.float32)
    dkeys = dkeys.reshape(img, local_width).astype(jnp.bfloat16)
    dvalues = jnp.einsum("kgsj,skgd->jkd", probs16, g_heads, preferred_element_type=jnp.float32)
    dvalues = dvalues.reshape(img, local_width).astype(jnp.bfloat16)
    dkeys_all, dvalues_all = (
        lax.all_gather(dkeys, "tensor", axis=1, tiled=True),
        lax.all_gather(dvalues, "tensor", axis=1, tiled=True),
    )
    contract_rows = (((0,), (0,)), ((), ()))
    key_acc = lax.dot_general(
        gathered, dkeys_all, contract_rows, preferred_element_type=jnp.float32
    )
    value_acc = lax.dot_general(
        gathered, dvalues_all, contract_rows, preferred_element_type=jnp.float32
    )
    contract_cols = (((1,), (1,)), ((), ()))
    feature_grad = lax.psum_scatter(
        lax.dot_general(dkeys_all, key_w, contract_cols, preferred_element_type=jnp.float32)
        + lax.dot_general(dvalues_all, value_w, contract_cols, preferred_element_type=jnp.float32),
        "section",
        scatter_dimension=0,
        tiled=True,
    ).astype(jnp.bfloat16)
    key_grad = key_acc.astype(jnp.bfloat16)[None]
    value_grad = value_acc.astype(jnp.bfloat16)[None]
    return (out[None], feature_grad, key_grad, value_grad)


def solution(mesh):
    in_specs = (
        P(("dp", "section"), "tensor"),
        P("section", "tensor", None),
        P("section", "tensor", None),
        P("section", "dp", "tensor"),
        P("section", "dp", "tensor"),
        P("dp"),
        P("dp"),
    )
    out_specs = (
        P("section", "dp", "tensor"),
        P(("dp", "section"), "tensor"),
        P("section", "tensor", "dp"),
        P("section", "tensor", "dp"),
    )
    return jax.shard_map(
        per_device, mesh=mesh, in_specs=in_specs, out_specs=out_specs, check_vma=False
    )
```

profile of v0, /device:TPU:64, one launch (start us, length us, event | category | flops | bytes accessed | tf_op | source)
XLA Modules:
  0.0 346.5 jit_solution(15868343676805438042)
XLA Ops:
  7.2 0.0 copy-start
  7.2 0.0 all-gather.4.cloned.1.call-start
  7.2 0.7 all-gather.4.cloned.1.call-update
  7.9 0.0 reduce-scatter.3.cloned.1.call-start
  8.0 33.2 %all-gather.4.cloned.1.call-done = bf16[768,1024]{1,0:T(8,128)(2,1)} async-done(((bf16[192,1024]{1,0:T(8,128)(2,1)}), bf16[768,1024]{1,0:T(8,128)(2,1)}) %all-gather.4.cloned.1.call-update) | async-done | bytes 1572880 | tf_op jit(solution)/shard_map/all_gather | solution.py:22
  41.2 4.0 %fusion.24 = f32[768,1,1024]{2,0,1:T(8,128)S(1)} fusion(bf16[768,1024]{1,0:T(8,128)(2,1)} %all-gather.4.cloned.1.call-done, bf16[1,1024,1024]{2,1,0:T(8,128)(2,1)} %param.8), kind=kOutput, calls=%fused_computation.29 | convolution fusion | flops 1610612736 | bytes 6815744 | tf_op jit(solution)/shard_map/dot_general | solution.py:25
  45.1 0.0 copy-done
  45.1 0.0 copy-done.6
  45.1 1.8 fusion.27
  47.0 3.2 pad_maximum_fusion
  50.2 0.0 reduce-scatter.3.cloned.1.call-update
  50.2 0.0 all-gather.8.cloned.1.call-start
  50.3 1.1 copy.32
  51.4 1.9 copy.33
  53.4 0.0 copy-done.5
  53.4 0.1 select_reduce_fusion
  53.5 0.0 copy-done.4
  53.5 0.3 convert_compare_fusion
  53.8 129.3 %reduce-scatter.3.cloned.1.call-done = f32[768,2,128]{2,0,1:T(8,128)} async-done(((f32[768,2,1024]{2,0,1:T(8,128)}), f32[768,2,128]{2,0,1:T(8,128)}) %reduce-scatter.3.cloned.1.call-update) | async-done | bytes 786448 | tf_op jit(solution)/shard_map/reduce_scatter | solution.py:30
  183.1 1.2 convert_element_type.57
  184.3 1.1 fusion.6
  185.4 0.0 copy-start.1
  185.4 0.0 copy-start.3
  185.4 1.3 fusion.5
  186.7 1.3 copy-done.1
  188.0 0.0 copy-done.3
  188.0 2.4 fusion.42
  190.4 0.0 all-gather.8.cloned.1.call-update
  190.5 0.0 all-gather.6.cloned.1.call-start
  190.5 0.0 copy-start.2
  190.5 4.4 %fusion = (f32[8,256]{1,0:T(8,128)S(1)}, f32[768,256,8]{1,0,2:T(8,128)S(1)}) fusion(f32[8,256]{1,0:T(8,128)S(1)} %fusion.5, f32[8,256]{1,0:T(8,128)S(1)} %get-tuple-element.12, f32[768,256,8]{1,0,2:T(8,128)} %copy-done.1, pred[256,768]{0,1:T(8,128)(4,1)S(1)} %convert_compare_fusion, bf16[256,8,128]{2,1,0:T(8,128)(2,1)} %bitcast.139, ...), kind=kOutput, calls=%fused_computation.4 | convolution fusion | flops 412088320 | bytes 13524992 | tf_op jit(solution)/shard_map/skgd,jkd->kgsj/dot_general | solution.py:54
  194.9 0.4 copy-done.2
  195.3 3.0 fusion.45
  198.3 0.0 all-gather.6.cloned.1.call-update
  198.3 0.2 reduce-scatter.5.cloned.1.call-start
  198.5 40.0 %all-gather.8.cloned.1.call-done = bf16[768,1024]{1,0:T(8,128)(2,1)} async-done(((bf16[768,128]{1,0:T(8,128)(2,1)}), bf16[768,1024]{1,0:T(8,128)(2,1)}) %all-gather.8.cloned.1.call-update) | async-done | bytes 1572880 | tf_op jit(solution)/shard_map/all_gather | solution.py:63
  238.5 4.9 %fusion.16 = f32[768,1024]{1,0:T(8,128)} fusion(bf16[768,1024]{1,0:T(8,128)(2,1)} %all-gather.8.cloned.1.call-done, bf16[1,1024,1024]{2,1,0:T(8,128)(2,1)S(1)} %copy-done), kind=kOutput, calls=%fused_computation.19 | convolution fusion | flops 1610612736 | bytes 6815744 | tf_op jit(solution)/shard_map/dot_general | solution.py:75
  243.5 45.8 %all-gather.6.cloned.1.call-done = bf16[768,1024]{1,0:T(8,128)(2,1)} async-done(((bf16[768,128]{1,0:T(8,128)(2,1)}), bf16[768,1024]{1,0:T(8,128)(2,1)}) %all-gather.6.cloned.1.call-update) | async-done | bytes 1572880 | tf_op jit(solution)/shard_map/all_gather | solution.py:62
  289.3 6.5 %fusion.30 = f32[768,1024]{1,0:T(8,128)} fusion(f32[768,1024]{1,0:T(8,128)} %fusion.16, bf16[768,1024]{1,0:T(8,128)(2,1)} %all-gather.6.cloned.1.call-done, bf16[1,1024,1024]{2,1,0:T(8,128)(2,1)} %param.8), kind=kOutput, calls=%fused_computation.31 | convolution fusion | flops 1611399168 | bytes 9961472 | tf_op jit(solution)/shard_map/dot_general | solution.py:74
  295.8 0.0 reduce-scatter.5.cloned.1.call-update
  295.8 4.6 %fusion.33 = bf16[128,8,256]{2,0,1:T(8,128)(2,1)S(1)} fusion(bf16[768,2,128]{2,0,1:T(8,128)(2,1)S(1)} %convert_element_type.57, f32[8,256]{1,0:T(8,128)S(1)} %fusion.5, f32[8,256]{1,0:T(8,128)S(1)} %get-tuple-element.12, f32[768,256,8]{1,0,2:T(8,128)} %copy-done.1, pred[256,768]{0,1:T(8,128)(4,1)S(1)} %convert_compare_fusion), kind=kOutput, calls=%fused_computation.32 | convolution fusion | flops 410779648 | bytes 7225344 | tf_op jit(solution)/shard_map/kgsj,jkd->skgd/dot_general | solution.py:51
  300.5 1.0 copy.26
  301.5 5.0 %convert_bitcast_fusion.1 = bf16[1,1024,1024]{1,2,0:T(8,128)(2,1)} fusion(bf16[768,1024]{1,0:T(8,128)(2,1)} %all-gather.6.cloned.1.call-done, bf16[768,1024]{1,0:T(8,128)(2,1)} %all-gather.4.cloned.1.call-done), kind=kOutput, calls=%fused_computation.28 | convolution fusion | flops 1611661312 | bytes 5242880 | tf_op jit(solution)/shard_map/dot_general | solution.py:66
  306.5 4.0 %copy.27 = bf16[1,1024,1024]{2,1,0:T(8,128)(2,1)} copy(bf16[1,1024,1024]{1,2,0:T(8,128)(2,1)} %convert_bitcast_fusion.1) | data formatting | bytes 4194304
  310.5 5.1 %convert_bitcast_fusion = bf16[1,1024,1024]{1,2,0:T(8,128)(2,1)} fusion(bf16[768,1024]{1,0:T(8,128)(2,1)} %all-gather.8.cloned.1.call-done, bf16[768,1024]{1,0:T(8,128)(2,1)} %all-gather.4.cloned.1.call-done), kind=kOutput, calls=%fused_computation.27 | convolution fusion | flops 1611661312 | bytes 5242880 | tf_op jit(solution)/shard_map/dot_general | solution.py:69
  315.6 3.9 %copy.28 = bf16[1,1024,1024]{2,1,0:T(8,128)(2,1)} copy(bf16[1,1024,1024]{1,2,0:T(8,128)(2,1)} %convert_bitcast_fusion) | data formatting | bytes 4194304
  319.5 18.5 %reduce-scatter.5.cloned.1.call-done = f32[192,1024]{1,0:T(8,128)} async-done(((f32[768,1024]{1,0:T(8,128)}), f32[192,1024]{1,0:T(8,128)}) %reduce-scatter.5.cloned.1.call-update) | async-done | bytes 786448 | tf_op jit(solution)/shard_map/reduce_scatter | solution.py:73
  338.0 1.9 convert_element_type.67
  (5 shorter events, 0.0 us)
Async XLA Ops:
  7.2 38.0 %copy-start = (bf16[1,1024,1024]{2,1,0:T(8,128)(2,1)S(1)}, bf16[1,1024,1024]{2,1,0:T(8,128)(2,1)}, u32[]{:S(2)}) copy-start(bf16[1,1024,1024]{2,1,0:T(8,128)(2,1)} %param.9) | copy-start | bytes 6291460
  7.2 34.0 %all-gather.4.cloned.1.call-start = ((), (), s32[]{:S(2)}) async-start(), calls=%async_computation.2 | async-start | bytes 1966080 | tf_op jit(solution)/shard_map/all_gather | solution.py:22
  7.9 175.2 %reduce-scatter.3.cloned.1.call-start = ((), (), s32[]{:S(2)}) async-start(), calls=%async_computation.3 | async-start | bytes 7077888 | tf_op jit(solution)/shard_map/reduce_scatter | solution.py:30
  41.2 4.0 %copy-start.6 = (bf16[768,1024]{1,0:T(8,128)(2,1)S(1)}, bf16[768,1024]{1,0:T(8,128)(2,1)}, u32[]{:S(2)}) copy-start(bf16[768,1024]{1,0:T(8,128)(2,1)} %all-gather.4.cloned.1.call-done) | copy-start | bytes 4718596
  50.2 3.2 copy-start.5
  50.2 3.3 copy-start.4
  50.2 188.3 %all-gather.8.cloned.1.call-start = ((), (), s32[]{:S(2)}) async-start(), calls=%async_computation.5 | async-start | bytes 1769472 | tf_op jit(solution)/shard_map/all_gather | solution.py:63
  185.4 2.7 copy-start.1
  185.4 2.7 copy-start.3
  190.5 98.8 %all-gather.6.cloned.1.call-start = ((), (), s32[]{:S(2)}) async-start(), calls=%async_computation.4 | async-start | bytes 1769472 | tf_op jit(solution)/shard_map/all_gather | solution.py:62
  190.5 4.8 %copy-start.2 = (f32[768,256,8]{1,0,2:T(8,128)S(1)}, f32[768,256,8]{1,0,2:T(8,128)}, u32[]{:S(2)}) copy-start(f32[768,256,8]{1,0,2:T(8,128)} %copy-done.1) | copy-start | bytes 18874372
  198.3 139.7 %reduce-scatter.5.cloned.1.call-start = ((), (), s32[]{:S(2)}) async-start(), calls=%async_computation.6 | async-start | bytes 3932160 | tf_op jit(solution)/shard_map/reduce_scatter | solution.py:73
Sparse Core Ops, SparseCore 0:
  9.8 31.2 all-gather.3
  50.4 132.7 reduce-scatter.2
  190.6 47.9 all-gather.7
  240.7 48.5 all-gather.5
  295.9 42.0 reduce-scatter.4
where the time goes:
time: 349 us; the launch traced here: 346 us
  waiting for transfers between devices  268 us (77%)
  matrix products  42.9 us (12%)
  between operations  13.9 us (4%)
  local copies, waits for them, and re-layouts  13.7 us (4%)
  other arithmetic  8.03 us (2%)
    reduce_scatter x1, waiting for transfers between devices, per_device(): lax.psum_scatter(partial_sums, 'tensor', scatter_dimension=2, tiled=True)  129 us
    all_gather x1, waiting for transfers between devices, per_device(): lax.all_gather(dkeys, 'tensor', axis=1, tiled=True)  45.8 us
    all_gather x1, waiting for transfers between devices, per_device(): lax.all_gather(dvalues, 'tensor', axis=1, tiled=True)  40 us
    all_gather x1, waiting for transfers between devices, per_device(): gathered = lax.all_gather(features, 'section', axis=0, tiled=True)  33.2 us
    reduce_scatter x1, waiting for transfers between devices, per_device(): lax.psum_scatter(lax.dot_general(dkeys_all, key_w, contract_cols, preferr...  18.5 us
    unnamed x19, local copies, waits for them, and re-layouts  13.7 us
  transfers between devices with their start and end apart: 5, of which 5 were waited for; matrix products, arithmetic and copies ran while one was open for 11% of the time, Pallas kernels for 0%

commit v1 on v0

v1 whole, which is shorter than its diff:
```python
import functools

import jax
import jax.numpy as jnp
from jax import lax
from jax.experimental import pallas as pl
from jax.experimental.pallas import tpu as pltpu
from jax.sharding import PartitionSpec as P

MESH = pl.DeviceIdType.MESH
F32 = jnp.float32
BF16 = jnp.bfloat16
I16 = jnp.int16
HD = 128
GROUP = 8
SECTIONS = 4
RING = 4
TILE = 192
CODED = TILE + 16
DEPTH = 1024
SEQ = 256
LEVELS = 32700.0
VMEM_LIMIT = 56 * 2**20


def place():
    t = lax.axis_index("tensor")
    return lax.axis_index("section"), lax.axis_index("dp"), t // 2, lax.rem(t, 2)


def along_x(d):
    s, dp, y, z = place()
    return (lax.rem(s + d, SECTIONS), dp, y * 2 + z)


def along_y(d):
    s, dp, y, z = place()
    return (s, dp, lax.rem(y + d, RING) * 2 + z)


def along_z():
    s, dp, y, z = place()
    return (s, dp, y * 2 + (1 - z))


def meet():
    barrier = pltpu.get_barrier_semaphore()
    peers = [along_x(d) for d in (1, 2, 3)] + [along_y(d) for d in (1, 2, 3)] + [along_z()]
    for peer in peers:
        pl.semaphore_signal(barrier, inc=1, device_id=peer, device_id_type=MESH)
    pl.semaphore_wait(barrier, len(peers))


def remote(src, dst, send_sem, recv_sem, device):
    return pltpu.make_async_remote_copy(
        src_ref=src, dst_ref=dst, send_sem=send_sem, recv_sem=recv_sem,
        device_id=device, device_id_type=MESH,
    )


def encode(x):
    top = jnp.maximum(jnp.max(jnp.abs(x), axis=0, keepdims=True), 1e-30)
    power = jnp.ceil(jnp.log(top) * 1.4426950408889634 + 0.0005)
    code = jnp.round(x * (jnp.exp2(-power) * LEVELS)).astype(jnp.int32).astype(I16)
    mark = jnp.broadcast_to(power, (16, x.shape[1])).astype(jnp.int32).astype(I16)
    return code, mark


def put(ref, at, x):
    code, mark = encode(x)
    ref[at + (slice(0, TILE), slice(None))] = code
    ref[at + (slice(TILE, CODED), slice(None))] = mark


def get(ref, at):
    code = ref[at + (slice(0, TILE), slice(None))].astype(jnp.int32).astype(F32)
    mark = ref[at + (slice(TILE, CODED), slice(None))].astype(jnp.int32).astype(F32)
    return code * (jnp.exp2(mark[:1]) * (1.0 / LEVELS))


def project_kernel(
    f_ref, wk_ref, wv_ref, keys_ref, values_ref, ft_ref,
    fg, pk, pv, kz_out, kz_in, ky_out, ky_in, vy_out, vy_in, vz_out, vz_in, sv,
    x_send, x_recv, kz_send, kz_recv, ky_send, ky_recv, vy_send, vy_recv, vz_send, vz_recv,
):
    s, dp, y, z = place()
    meet()
    sends = []
    gathers = {}
    for d in (1, 3, 2):
        k = SECTIONS - d
        gathers[k] = remote(f_ref, fg.at[k], x_send.at[k], x_recv.at[k], along_x(d))
        gathers[k].start()
        sends.append(gathers[k])

    first_k, first_v, second_k, second_v = {}, {}, {}, {}

    def start(k):
        if k:
            gathers[k].wait_recv()
            tile = fg[k]
        else:
            tile = f_ref[...]
        v = jnp.dot(tile, wv_ref[...], preferred_element_type=F32)
        for h in range(8):
            pv[k, h] = v[:, h * HD:(h + 1) * HD]
        for d in (2, 1, 3):
            for r in range(2):
                head = lax.rem(y + d, RING) * 2 + lax.rem(z + r, 2)
                put(vy_out, (k, d, r), pv[k, head])
            copy = remote(
                vy_out.at[k, d], vy_in.at[k, RING - d],
                vy_send.at[k, d], vy_recv.at[k, RING - d], along_y(d),
            )
            copy.start()
            first_v[k, d] = copy
            sends.append(copy)
        q = jnp.dot(tile, wk_ref[...], preferred_element_type=F32)
        for h in range(8):
            pk[k, h] = q[:, h * HD:(h + 1) * HD]
        for d in range(RING):
            head = lax.rem(y + d, RING) * 2 + (1 - z)
            put(kz_out, (k, d), pk[k, head])
        copy = remote(kz_out.at[k], kz_in.at[k], kz_send.at[k], kz_recv.at[k], along_z())
        copy.start()
        first_k[k] = copy
        sends.append(copy)
        ft_ref[k] = tile.T

    def middle(k):
        first_k[k].wait_recv()
        for d in (2, 1, 3, 0):
            head = lax.rem(y + d, RING) * 2 + z
            total = pk[k, head] + get(kz_in, (k, d))
            if d:
                put(ky_out, (k, d), total)
                copy = remote(
                    ky_out.at[k, d], ky_in.at[k, RING - d],
                    ky_send.at[k, d], ky_recv.at[k, RING - d], along_y(d),
                )
                copy.start()
                second_k[k, d] = copy
                sends.append(copy)
            else:
                pk[k, head] = total
        for d in (1, 3, 2):
            first_v[k, RING - d].wait_recv()
        for r in (1, 0):
            head = y * 2 + lax.rem(z + r, 2)
            total = pv[k, head]
            for d in (1, 2, 3):
                total = total + get(vy_in, (k, d, r))
            if r:
                put(vz_out, (k,), total)
                copy = remote(vz_out.at[k], vz_in.at[k], vz_send.at[k], vz_recv.at[k], along_z())
                copy.start()
                second_v[k] = copy
                sends.append(copy)
            else:
                sv[k] = total

    def finish(k):
        for d in (1, 3, 2):
            second_k[k, RING - d].wait_recv()
        total = pk[k, y * 2 + z]
        for d in (1, 2, 3):
            total = total + get(ky_in, (k, d))
        keys_ref[k] = total.astype(BF16)
        second_v[k].wait_recv()
        values_ref[k] = (sv[k] + get(vz_in, (k,))).astype(BF16)

    order = (0, 1, 3, 2)
    for i in range(len(order) + 2):
        if i < len(order):
            start(order[i])
        if 0 <= i - 1 < len(order):
            middle(order[i - 1])
        if 0 <= i - 2:
            finish(order[i - 2])
    for copy in sends:
        copy.wait_send()


def project(f, wk, wv):
    dma = pltpu.SemaphoreType.DMA
    return pl.pallas_call(
        project_kernel,
        out_shape=(
            jax.ShapeDtypeStruct((4, TILE, HD), BF16),
            jax.ShapeDtypeStruct((4, TILE, HD), BF16),
            jax.ShapeDtypeStruct((4, DEPTH, TILE), BF16),
        ),
        in_specs=[pl.BlockSpec(memory_space=pltpu.VMEM)] * 3,
        out_specs=(pl.BlockSpec(memory_space=pltpu.VMEM),) * 3,
        scratch_shapes=[
            pltpu.VMEM((4, TILE, DEPTH), BF16),
            pltpu.VMEM((4, 8, TILE, HD), F32),
            pltpu.VMEM((4, 8, TILE, HD), F32),
            pltpu.VMEM((4, 4, CODED, HD), I16),
            pltpu.VMEM((4, 4, CODED, HD), I16),
            pltpu.VMEM((4, 4, CODED, HD), I16),
            pltpu.VMEM((4, 4, CODED, HD), I16),
            pltpu.VMEM((4, 4, 2, CODED, HD), I16),
            pltpu.VMEM((4, 4, 2, CODED, HD), I16),
            pltpu.VMEM((4, CODED, HD), I16),
            pltpu.VMEM((4, CODED, HD), I16),
            pltpu.VMEM((4, TILE, HD), F32),
            dma((4,)), dma((4,)),
            dma((4,)), dma((4,)),
            dma((4, 4)), dma((4, 4)),
            dma((4, 4)), dma((4, 4)),
            dma((4,)), dma((4,)),
        ],
        compiler_params=pltpu.CompilerParams(
            collective_id=1, has_side_effects=True, vmem_limit_bytes=VMEM_LIMIT
        ),
        name="project",
    )(f, wk, wv)


def attend_kernel(q_ref, g_ref, k_ref, v_ref, lim_ref, last_ref, out_ref, dk_ref, dv_ref, acc_k, acc_v):
    scale = HD ** -0.5
    rows = 4 * TILE
    keys = k_ref[...]
    values = v_ref[...]
    values_t = values.T
    visible = lim_ref[...] <= last_ref[...]
    across = (((1,), (1,)), ((), ()))
    for h in range(GROUP):
        cols = slice(h * HD, (h + 1) * HD)
        q = q_ref[:, cols]
        g = g_ref[:, cols]
        scores = lax.dot_general(keys, q, across, preferred_element_type=F32) * scale
        masked = jnp.where(visible, scores, -jnp.inf)
        top = jnp.max(masked, axis=0, keepdims=True)
        expo = jnp.exp(masked - top)
        probs = expo * (1.0 / jnp.sum(expo, axis=0, keepdims=True))
        probs16 = probs.astype(BF16)
        out_t = jnp.dot(values_t, probs16, preferred_element_type=F32)
        out_ref[:, cols] = out_t.T.astype(BF16)
        dprobs = lax.dot_general(values, g, across, preferred_element_type=F32)
        delta = jnp.sum(probs * dprobs, axis=0, keepdims=True)
        dscores = (probs * (dprobs - delta) * scale).astype(BF16)
        dv = jnp.dot(probs16, g, preferred_element_type=F32)
        dk = jnp.dot(dscores, q, preferred_element_type=F32)
        if h == 0:
            acc_k[...] = dk
            acc_v[...] = dv
        else:
            acc_k[...] += dk
            acc_v[...] += dv
    dk_ref[...] = acc_k[...].astype(BF16)
    dv_ref[...] = acc_v[...].astype(BF16)


def attend(q, g, keys, values, lim, last):
    rows = 4 * TILE
    return pl.pallas_call(
        attend_kernel,
        out_shape=(
            jax.ShapeDtypeStruct((SEQ, GROUP * HD), BF16),
            jax.ShapeDtypeStruct((rows, HD), BF16),
            jax.ShapeDtypeStruct((rows, HD), BF16),
        ),
        in_specs=[pl.BlockSpec(memory_space=pltpu.VMEM)] * 6,
        out_specs=(pl.BlockSpec(memory_space=pltpu.VMEM),) * 3,
        scratch_shapes=[pltpu.VMEM((rows, HD), F32), pltpu.VMEM((rows, HD), F32)],
        compiler_params=pltpu.CompilerParams(vmem_limit_bytes=VMEM_LIMIT),
        name="attend",
    )(q, g, keys, values, lim, last)


def spread_kernel(
    dk_ref, dv_ref, ft_ref, wk_ref, wv_ref, fgrad_ref, kgrad_ref, vgrad_ref,
    gk, gv, fs, fr, acc_f, acc_k, acc_v,
    own, k1s, k1r, k2s, k2r, v1s, v1r, v2s, v2r, zs, zr, xs, xr,
):
    s, dp, y, z = place()
    me = y * 2 + z

    def cols(head):
        return pl.ds(pl.multiple_of(head * HD, HD), HD)

    mine = cols(me)
    mate = cols(y * 2 + (1 - z))
    meet()
    sends = []
    owned, near, seen = {}, {}, {}

    def first(k):
        for j, (src, dst) in enumerate(((dk_ref, gk), (dv_ref, gv))):
            copy = pltpu.make_async_copy(src.at[k], dst.at[k, :, mine], own.at[k, j])
            copy.start()
            owned[k, j] = copy
        copy = remote(dk_ref.at[k], gk.at[k, :, mine], zs.at[k, 0], zr.at[k, 0], along_z())
        copy.start()
        near[k, "z"] = copy
        for d in (2, 1, 3):
            copy = remote(dv_ref.at[k], gv.at[k, :, mine], v1s.at[k, d], v1r.at[k, RING - d], along_y(d))
            copy.start()
            near[k, RING - d] = copy
        for d in (2, 1, 3):
            copy = remote(dk_ref.at[k], gk.at[k, :, mine], k1s.at[k, d], k1r.at[k, RING - d], along_y(d))
            copy.start()
            seen[k, "k1", RING - d] = copy
        copy = remote(dv_ref.at[k], gv.at[k, :, mine], zs.at[k, 1], zr.at[k, 1], along_z())
        copy.start()
        seen[k, "z1"] = copy

    def second(k):
        near[k, "z"].wait_recv()
        for d in (2, 1, 3):
            copy = remote(gk.at[k, :, mate], gk.at[k, :, mate], k2s.at[k, d], k2r.at[k, RING - d], along_y(d))
            copy.start()
            seen[k, "k2", RING - d] = copy
        for d in (1, 3, 2):
            near[k, d].wait_recv()
            head = cols(lax.rem(y + d, RING) * 2 + z)
            copy = remote(gv.at[k, :, head], gv.at[k, :, head], v2s.at[k, d], v2r.at[k, d], along_z())
            copy.start()
            seen[k, "v2", d] = copy

    across = (((1,), (1,)), ((), ()))
    parts = []

    def third(k, begin):
        owned[k, 0].wait()
        owned[k, 1].wait()
        for name, copy in seen.items():
            if name[0] == k:
                copy.wait_recv()
        total = lax.dot_general(gk[k], wk_ref[...], across, preferred_element_type=F32)
        total += lax.dot_general(gv[k], wv_ref[...], across, preferred_element_type=F32)
        if k:
            fs[k] = total.astype(BF16)
            copy = remote(fs.at[k], fr.at[SECTIONS - k], xs.at[k], xr.at[SECTIONS - k], along_x(k))
            copy.start()
            parts.append(copy)
        else:
            acc_f[...] = total
        kw = jnp.dot(ft_ref[k], gk[k], preferred_element_type=F32)
        vw = jnp.dot(ft_ref[k], gv[k], preferred_element_type=F32)
        if begin:
            acc_k[...] = kw
            acc_v[...] = vw
        elif k:
            acc_k[...] += kw
            acc_v[...] += vw
        else:
            kgrad_ref[...] = (acc_k[...] + kw).astype(BF16)
            vgrad_ref[...] = (acc_v[...] + vw).astype(BF16)

    order = (2, 1, 3, 0)
    n = len(order)
    first(order[0])
    first(order[1])
    second(order[0])
    for i in range(n):
        if i + 2 < n:
            first(order[i + 2])
        if i + 1 < n:
            second(order[i + 1])
        third(order[i], i == 0)
    for copy in parts:
        copy.wait_recv()
    total = acc_f[...]
    for k in (1, 2, 3):
        total = total + fr[k].astype(F32)
    fgrad_ref[...] = total.astype(BF16)
    for copy in list(near.values()) + list(seen.values()) + parts:
        copy.wait_send()


def spread(dk, dv, ft, wk, wv):
    dma = pltpu.SemaphoreType.DMA
    return pl.pallas_call(
        spread_kernel,
        out_shape=(
            jax.ShapeDtypeStruct((TILE, DEPTH), BF16),
            jax.ShapeDtypeStruct((DEPTH, GROUP * HD), BF16),
            jax.ShapeDtypeStruct((DEPTH, GROUP * HD), BF16),
        ),
        in_specs=[pl.BlockSpec(memory_space=pltpu.VMEM)] * 5,
        out_specs=(pl.BlockSpec(memory_space=pltpu.VMEM),) * 3,
        scratch_shapes=[
            pltpu.VMEM((4, TILE, GROUP * HD), BF16),
            pltpu.VMEM((4, TILE, GROUP * HD), BF16),
            pltpu.VMEM((4, TILE, DEPTH), BF16),
            pltpu.VMEM((4, TILE, DEPTH), BF16),
            pltpu.VMEM((TILE, DEPTH), F32),
            pltpu.VMEM((DEPTH, GROUP * HD), F32),
            pltpu.VMEM((DEPTH, GROUP * HD), F32),
            dma((4, 2)),
            dma((4, 4)), dma((4, 4)), dma((4, 4)), dma((4, 4)),
            dma((4, 4)), dma((4, 4)), dma((4, 4)), dma((4, 4)),
            dma((4, 2)), dma((4, 2)),
            dma((4,)), dma((4,)),
        ],
        compiler_params=pltpu.CompilerParams(
            collective_id=2, has_side_effects=True, vmem_limit_bytes=VMEM_LIMIT
        ),
        name="spread",
    )(dk, dv, ft, wk, wv)


def per_device(features, key_weight, value_weight, queries, out_grad, tile_count, tile_last):
    wk, wv = key_weight[0], value_weight[0]
    keys, values, ft = project(features, wk, wv)
    s = lax.axis_index("section")
    tiles = lax.rem(s + jnp.arange(4, dtype=jnp.int32), SECTIONS)
    counts = tile_count[tiles]
    slot = jnp.arange(TILE, dtype=jnp.int32)
    lim = jnp.where(slot[None, :] < counts[:, None], tiles[:, None], SECTIONS).reshape(4 * TILE, 1)
    out, dk, dv = attend(
        queries[0], out_grad[0], keys.reshape(4 * TILE, HD), values.reshape(4 * TILE, HD),
        lim, tile_last.reshape(1, SEQ),
    )
    fgrad, kgrad, vgrad = spread(
        dk.reshape(4, TILE, HD), dv.reshape(4, TILE, HD), ft, wk, wv
    )
    return (out[None], fgrad, kgrad[None], vgrad[None])


def solution(mesh):
    in_specs = (
        P(("dp", "section"), "tensor"),
        P("section", "tensor", None),
        P("section", "tensor", None),
        P("section", "dp", "tensor"),
        P("section", "dp", "tensor"),
        P("dp"),
        P("dp"),
    )
    out_specs = (
        P("section", "dp", "tensor"),
        P(("dp", "section"), "tensor"),
        P("section", "tensor", "dp"),
        P("section", "tensor", "dp"),
    )
    return jax.shard_map(
        per_device, mesh=mesh, in_specs=in_specs, out_specs=out_specs, check_vma=False
    )
```

time: 349 us -> 105 us (0.30)
  waiting for transfers between devices: 268 us -> 0 us
  Pallas kernels: 0 us -> 95.3 us
  matrix products: 42.9 us -> 0 us
  between operations: 13.9 us -> 0.68 us
  other arithmetic: 8.03 us -> 0.1 us
  local copies, waits for them, and re-layouts: 13.7 us -> 8.59 us
    reduce_scatter x2 -> x0, waiting for transfers between devices: 148 us -> none  [the longest x1 129 us: per_device(): lax.psum_scatter(partial_sums, 'tensor', scatter_dimension=2, tiled=True)]
    all_gather x3 -> x0, waiting for transfers between devices: 119 us -> none  [the longest x1 45.8 us: per_device(): lax.all_gather(dkeys, 'tensor', axis=1, tiled=True)]
    pallas_call x0 -> x3, Pallas kernels: none -> 95.3 us  [the longest x1 45.3 us: project(): pl.pallas_call(project_kernel, out_shape=(jax.ShapeDtypeStruct((4, TILE,...]
    dot_general x11 -> x0, matrix products: 42.9 us -> none  [the longest x1 6.53 us: per_device(): lax.dot_general(dkeys_all, key_w, contract_cols, preferred_element_type=j...]
    unnamed x19 -> x7, local copies, waits for them, and re-layouts: 13.7 us -> 6.92 us
  transfers between devices with their start and end apart: 5 -> 0, of which waited for: 5 -> 0; matrix products, arithmetic and copies ran while one was open for 11% -> 0% of each run, Pallas kernels for 0% -> 0%
where the time goes in v1:
time: 105 us
  Pallas kernels  95.3 us (91%)
  local copies, waits for them, and re-layouts  8.59 us (8%)
    pallas_call x1, Pallas kernels, project(): pl.pallas_call(project_kernel, out_shape=(jax.ShapeDtypeStruct((4, TILE,...  45.3 us
    pallas_call x1, Pallas kernels, spread(): pl.pallas_call(spread_kernel, out_shape=(jax.ShapeDtypeStruct((TILE, DEPT...  39.9 us
    pallas_call x1, Pallas kernels, attend(): pl.pallas_call(attend_kernel, out_shape=(jax.ShapeDtypeStruct((SEQ, GROUP...  10.1 us
    unnamed x7, local copies, waits for them, and re-layouts  6.92 us

profile of v1, /device:TPU:64, one launch (start us, length us, event | category | flops | bytes accessed | tf_op | source)
XLA Modules:
  0.0 104.7 jit_solution(9536249832305107080)
XLA Ops:
  0.6 0.0 copy-start
  0.7 0.6 copy-done
  1.3 0.6 gather_fusion
  1.9 0.1 fusion
  2.0 1.0 select_n.27.lim_ref
  3.0 45.3 %project.1 = (bf16[4,192,128]{2,1,0:T(8,128)(2,1)}, bf16[4,192,128]{2,1,0:T(8,128)(2,1)}, bf16[4,1024,192]{2,1,0:T(8,128)(2,1)}) custom-call(bf16[192,1024]{1,0:T(8,128)(2,1)} %f_ref.1, bf16[1024,1024]{1,0:T(8,128)(2,1)} %bitcast.14, bf16[1024,1024]{1,0:T(8,128)(2,1)} %bitcast.16), custom_call_target="tpu_custom_call" | custom-call | tf_op jit(solution)/shard_map/project/pallas_call | solution.py:186
  48.3 10.1 %attend.1 = (bf16[256,1024]{1,0:T(8,128)(2,1)}, bf16[768,128]{1,0:T(8,128)(2,1)}, bf16[768,128]{1,0:T(8,128)(2,1)}) custom-call(bf16[256,1024]{1,0:T(8,128)(2,1)} %bitcast.20, bf16[256,1024]{1,0:T(8,128)(2,1)} %bitcast.21, bf16[768,128]{1,0:T(8,128)(2,1)} %bitcast.24, bf16[768,128]{1,0:T(8,128)(2,1)} %bitcast.25, s32[768,1]{1,0:T(8,128)} %select_n.27.lim_ref, ...), custom_call_target="tpu_custom_call" | custom-call | tf_op jit(solution)/shard_map/attend/pallas_call | solution.py:258
  58.4 39.9 %spread.1 = (bf16[192,1024]{1,0:T(8,128)(2,1)}, bf16[1024,1024]{1,0:T(8,128)(2,1)}, bf16[1024,1024]{1,0:T(8,128)(2,1)}) custom-call(bf16[4,192,128]{2,1,0:T(8,128)(2,1)} %bitcast.22, bf16[4,192,128]{2,1,0:T(8,128)(2,1)} %bitcast.23, bf16[4,1024,192]{2,1,0:T(8,128)(2,1)} %get-tuple-element.18.ft_ref, bf16[1024,1024]{1,0:T(8,128)(2,1)} %bitcast.15, ...), custom_call_target="tpu_custom_call" | custom-call | tf_op jit(solution)/shard_map/spread/pallas_call | solution.py:376
  98.4 1.8 %copy.15 = bf16[192,1024]{1,0:T(8,128)(2,1)} copy(bf16[192,1024]{1,0:T(8,128)(2,1)} %get-tuple-element.27) | data formatting | bytes 786432
  100.1 0.0 copy-start.1
  100.1 3.2 %copy.16 = bf16[1,1024,1024]{2,1,0:T(8,128)(2,1)} copy(bf16[1,1024,1024]{2,1,0:T(8,128)(2,1)} %bitcast.19) | data formatting | bytes 4194304
  103.4 0.0 copy-done.1
  103.4 1.3 %copy.17 = bf16[1,1024,1024]{2,1,0:T(8,128)(2,1)} copy(bf16[1,1024,1024]{2,1,0:T(8,128)(2,1)S(1)} %bitcast.18) | data formatting | bytes 4194304
  (3 shorter events, 0.0 us)
Async XLA Ops:
  0.6 0.7 copy-start
  100.1 3.2 %copy-start.1 = (bf16[1024,1024]{1,0:T(8,128)(2,1)S(1)}, bf16[1024,1024]{1,0:T(8,128)(2,1)}, u32[]{:S(2)}) copy-start(bf16[1024,1024]{1,0:T(8,128)(2,1)} %get-tuple-element.21) | copy-start | bytes 6291460

commit v2 on v0

v2 whole, which is shorter than its diff:
```python
import functools

import jax
import jax.numpy as jnp
from jax import lax
from jax.experimental import pallas as pl
from jax.experimental.pallas import tpu as pltpu
from jax.sharding import PartitionSpec as P

MESH = pl.DeviceIdType.MESH
F32 = jnp.float32
BF16 = jnp.bfloat16
I16 = jnp.int16
HD = 128
GROUP = 8
SECTIONS = 4
RING = 4
TILE = 192
HALF = TILE // 2
DEPTH = 1024
SEQ = 256
LEVELS = 32700.0
FLOOR = -1e30
VMEM_LIMIT = 56 * 2**20


def place():
    t = lax.axis_index("tensor")
    return lax.axis_index("section"), lax.axis_index("dp"), t // 2, lax.rem(t, 2)


def along_x(d):
    s, dp, y, z = place()
    return (lax.rem(s + d, SECTIONS), dp, y * 2 + z)


def along_y(d):
    s, dp, y, z = place()
    return (s, dp, lax.rem(y + d, RING) * 2 + z)


def along_z():
    s, dp, y, z = place()
    return (s, dp, y * 2 + (1 - z))


def meet():
    barrier = pltpu.get_barrier_semaphore()
    peers = [along_x(d) for d in (1, 2, 3)] + [along_y(d) for d in (1, 2, 3)] + [along_z()]
    for peer in peers:
        pl.semaphore_signal(barrier, inc=1, device_id=peer, device_id_type=MESH)
    pl.semaphore_wait(barrier, len(peers))


def remote(src, dst, send_sem, recv_sem, device):
    return pltpu.make_async_remote_copy(
        src_ref=src, dst_ref=dst, send_sem=send_sem, recv_sem=recv_sem,
        device_id=device, device_id_type=MESH,
    )


def encode(x):
    top = jnp.maximum(jnp.max(jnp.abs(x), axis=0, keepdims=True), 1e-30)
    power = jnp.ceil(jnp.log(top) * 1.4426950408889634 + 0.0005)
    code = jnp.round(x * (jnp.exp2(-power) * LEVELS)).astype(jnp.int32).astype(I16)
    return code, power


def marks(powers):
    row = lax.broadcasted_iota(jnp.int32, (16, HD), 0)
    mark = jnp.broadcast_to(powers[0], (16, HD))
    for i, power in enumerate(powers[1:]):
        mark = jnp.where(row == i + 1, power, mark)
    return mark.astype(jnp.int32).astype(I16)


def units(mark):
    return jnp.exp2(mark.astype(jnp.int32).astype(F32)) * (1.0 / LEVELS)


def as_f32(code):
    return code.astype(jnp.int32).astype(F32)


ACROSS = (((1,), (1,)), ((), ()))
CHUNKS = ((0, 0), (0, 1), (1, 0), (3, 0), (1, 1), (3, 1), (2, 0), (2, 1))
TILES = (2, 1, 3, 0)


def main_kernel(
    count_ref, last_ref, f_ref, wk_ref, wv_ref, q_ref, g_ref,
    gk_out, gv_out, ft_out, att_out, fgrad_out,
    fg, wk, wv, q, g, pk, pv, kz_out, kz_in, ky_out, ky_in, vy_out, vy_in, vz_out, vz_in, sv,
    keys, values, expo, dprobs, tops, sums, dots, probs, dscores, dks, dvs, gk, gv, fs, fr, acc,
    ft, att, fgrad,
    load, store, own, x_send, x_recv, kz_send, kz_recv, ky_send, ky_recv,
    vy_send, vy_recv, vz_send, vz_recv,
    az_s, az_r, as_s, as_r, a2_s, a2_r, by_s, by_r, b2_s, b2_r, bz_s, bz_r, fx_s, fx_r,
):
    s, dp, y, z = place()
    scale = HD ** -0.5
    loads = [
        pltpu.make_async_copy(src, dst, load.at[i])
        for i, (src, dst) in enumerate(
            ((f_ref, fg.at[0]), (wv_ref, wv), (wk_ref, wk), (q_ref, q), (g_ref, g))
        )
    ]
    for copy in loads:
        copy.start()
    meet()
    sends = []

    def go(*args):
        copy = remote(*args)
        copy.start()
        sends.append(copy)
        return copy

    def half(k, h):
        return fg.at[k, pl.ds(h * HALF, HALF)]

    loads[0].wait()
    gathers = {}
    for h in range(2):
        for d in (1, 3):
            k = SECTIONS - d
            gathers[k, h] = go(half(0, h), half(k, h), x_send.at[k, h], x_recv.at[k, h], along_x(d))

    first_k, first_v, second_k, second_v = {}, {}, {}, {}

    def head_at(d, r):
        return lax.rem(y + d, RING) * 2 + lax.rem(z + r, 2)

    def start(i):
        k, h = CHUNKS[i]
        if k:
            gathers[k, h].wait_recv()
        if (k, h) == (1, 0):
            gathers[2, 0] = go(half(1, 0), half(2, 0), x_send.at[2, 0], x_recv.at[2, 0], along_x(3))
        if (k, h) == (3, 1):
            gathers[2, 1] = go(half(3, 1), half(2, 1), x_send.at[2, 1], x_recv.at[2, 1], along_x(1))
        if i == 0:
            loads[1].wait()
        rows = fg[k, h * HALF:(h + 1) * HALF, :]
        v = jnp.dot(rows, wv[...], preferred_element_type=F32)
        for head in range(8):
            pv[i, head] = v[:, head * HD:(head + 1) * HD]
        for d in (2, 1, 3):
            for r in range(2):
                vy_out[i, d, r] = pv[i, head_at(d, r)].astype(BF16)
            first_v[i, d] = go(
                vy_out.at[i, d], vy_in.at[i, RING - d],
                vy_send.at[i, d], vy_recv.at[i, RING - d], along_y(d),
            )
        if i == 0:
            loads[2].wait()
        p = jnp.dot(rows, wk[...], preferred_element_type=F32)
        for head in range(8):
            pk[i, head] = p[:, head * HD:(head + 1) * HD]
        powers = []
        for d in range(RING):
            code, power = encode(pk[i, head_at(d, 1)])
            kz_out[i, d * HALF:(d + 1) * HALF, :] = code
            powers.append(power)
        kz_out[i, 4 * HALF:4 * HALF + 16, :] = marks(powers)
        first_k[i] = go(kz_out.at[i], kz_in.at[i], kz_send.at[i], kz_recv.at[i], along_z())

    def middle(i):
        first_k[i].wait_recv()
        unit = units(kz_in[i, 4 * HALF:4 * HALF + 16, :])
        for d in (2, 1, 3, 0):
            head = head_at(d, 0)
            total = pk[i, head] + as_f32(kz_in[i, d * HALF:(d + 1) * HALF, :]) * unit[d:d + 1]
            if d:
                code, power = encode(total)
                ky_out[i, d, 0:HALF, :] = code
                ky_out[i, d, HALF:HALF + 16, :] = marks([power])
                second_k[i, d] = go(
                    ky_out.at[i, d], ky_in.at[i, RING - d],
                    ky_send.at[i, d], ky_recv.at[i, RING - d], along_y(d),
                )
            else:
                pk[i, head] = total
        for d in (1, 3, 2):
            first_v[i, RING - d].wait_recv()
        for r in (1, 0):
            total = pv[i, head_at(0, r)]
            for d in (1, 2, 3):
                total = total + vy_in[i, d, r].astype(F32)
            if r:
                vz_out[i] = total.astype(BF16)
                second_v[i] = go(vz_out.at[i], vz_in.at[i], vz_send.at[i], vz_recv.at[i], along_z())
            else:
                sv[i] = total

    def finish(i):
        k, h = CHUNKS[i]
        spot = slice(k * TILE + h * HALF, k * TILE + (h + 1) * HALF)
        for d in (1, 3, 2):
            second_k[i, RING - d].wait_recv()
        total = pk[i, head_at(0, 0)]
        for d in (1, 2, 3):
            unit = units(ky_in[i, d, HALF:HALF + 16, :])
            total = total + as_f32(ky_in[i, d, 0:HALF, :]) * unit[0:1]
        key = total.astype(BF16)
        keys[spot, :] = key
        second_v[i].wait_recv()
        value = (sv[i] + vz_in[i].astype(F32)).astype(BF16)
        values[spot, :] = value
        tile = lax.rem(s + k, SECTIONS)
        slot = lax.broadcasted_iota(jnp.int32, (HALF, SEQ), 0) + h * HALF
        limit = jnp.where(slot < count_ref[tile], tile, SECTIONS)
        visible = limit <= last_ref[...]
        for j in range(GROUP):
            cols = slice(j * HD, (j + 1) * HD)
            wide = slice(j * SEQ, (j + 1) * SEQ)
            scores = lax.dot_general(key, q[:, cols], ACROSS, preferred_element_type=F32) * scale
            masked = jnp.where(visible, scores, -jnp.inf)
            top = jnp.maximum(jnp.max(masked, axis=0, keepdims=True), FLOOR)
            e = jnp.exp(masked - top)
            dprob = lax.dot_general(value, g[:, cols], ACROSS, preferred_element_type=F32)
            expo[spot, wide] = e
            dprobs[spot, wide] = dprob
            tops[i:i + 1, wide] = top
            sums[i:i + 1, wide] = jnp.sum(e, axis=0, keepdims=True)
            dots[i:i + 1, wide] = jnp.sum(e * dprob, axis=0, keepdims=True)

    def turn(a):
        ft[:, a * 2 * TILE:(a + 1) * 2 * TILE] = jnp.concatenate([fg[2 * a], fg[2 * a + 1]], axis=0).T
        copy = pltpu.make_async_copy(
            ft.at[:, pl.ds(a * 2 * TILE, 2 * TILE)], ft_out.at[:, pl.ds(a * 2 * TILE, 2 * TILE)],
            store.at[a],
        )
        copy.start()
        return copy

    stores = []
    n = len(CHUNKS)
    for i in range(n + 2):
        if i < n:
            start(i)
        if 0 <= i - 1 < n:
            middle(i - 1)
        if i == 2:
            loads[3].wait()
            loads[4].wait()
        if 0 <= i - 2:
            finish(i - 2)
        if i == 5:
            stores.append(turn(0))

    peak = jnp.max(tops[...], axis=0, keepdims=True)
    share = jnp.exp(tops[...] - peak)
    inverse = 1.0 / jnp.sum(share * sums[...], axis=0, keepdims=True)
    share = share * inverse
    sums[...] = share
    dots[0:1, :] = jnp.sum(share * dots[...], axis=0, keepdims=True)

    def cols(head, n=1):
        return pl.ds(pl.multiple_of(head * HD, HD), n * HD)

    mine = cols(y * 2 + z)
    owned, az, ae, a2, by, b2, bz = {}, {}, {}, {}, {}, {}, {}

    def attend(k):
        dk = dv = None
        for j in range(GROUP):
            narrow = slice(j * HD, (j + 1) * HD)
            wide = slice(j * SEQ, (j + 1) * SEQ)
            delta = dots[0:1, wide]
            for h in range(2):
                i = CHUNKS.index((k, h))
                spot = slice(k * TILE + h * HALF, k * TILE + (h + 1) * HALF)
                p = expo[spot, wide] * sums[i:i + 1, wide]
                probs[spot, wide] = p.astype(BF16)
                dscores[h * HALF:(h + 1) * HALF, wide] = (p * (dprobs[spot, wide] - delta) * scale).astype(BF16)
            whole = slice(k * TILE, (k + 1) * TILE)
            dv_j = jnp.dot(probs[whole, wide], g[:, narrow], preferred_element_type=F32)
            dk_j = jnp.dot(dscores[:, wide], q[:, narrow], preferred_element_type=F32)
            dv = dv_j if j == 0 else dv + dv_j
            dk = dk_j if j == 0 else dk + dk_j
        dvs[k] = dv.astype(BF16)
        dks[k] = dk.astype(BF16)

    def ways(k):
        return (1, 3) if TILES.index(k) % 2 == 0 else (3, 1)

    def zero(k):
        attend(k)
        by[k, 3] = go(dvs.at[k], gv.at[k, :, mine], by_s.at[k, 1], by_r.at[k, 3], along_y(1))
        by[k, 1] = go(dvs.at[k], gv.at[k, :, mine], by_s.at[k, 3], by_r.at[k, 1], along_y(3))
        az[k] = go(dks.at[k], gk.at[k, :, mine], az_s.at[k], az_r.at[k], along_z())
        bz[k, 0] = go(dvs.at[k], gv.at[k, :, mine], bz_s.at[k, 0], bz_r.at[k, 0], along_z())
        for j, (src, dst) in enumerate(((dks, gk), (dvs, gv))):
            copy = pltpu.make_async_copy(src.at[k], dst.at[k, :, mine], own.at[k, j])
            copy.start()
            owned[k, j] = copy

    def one(k):
        ahead, behind = ways(k)
        owned[k, 0].wait()
        az[k].wait_recv()
        pair = cols(y * 2, 2)
        for d in (1, 3):
            ae[k, RING - d] = go(
                gk.at[k, :, pair], gk.at[k, :, pair],
                as_s.at[k, d], as_r.at[k, RING - d], along_y(d),
            )
        for d in (behind, ahead):
            by[k, d].wait_recv()
            head = cols(head_at(d, 0))
            if d == behind:
                b2[k] = go(gv.at[k, :, head], gv.at[k, :, head], b2_s.at[k], b2_r.at[k], along_y(ahead))
            bz[k, d] = go(gv.at[k, :, head], gv.at[k, :, head], bz_s.at[k, d], bz_r.at[k, d], along_z())

    def two(k):
        ahead, behind = ways(k)
        ae[k, behind].wait_recv()
        pair = cols(lax.rem(y + behind, RING) * 2, 2)
        a2[k] = go(gk.at[k, :, pair], gk.at[k, :, pair], a2_s.at[k], a2_r.at[k], along_y(ahead))
        b2[k].wait_recv()
        head = cols(head_at(2, 0))
        bz[k, 2] = go(gv.at[k, :, head], gv.at[k, :, head], bz_s.at[k, 2], bz_r.at[k, 2], along_z())

    parts = []

    def three(k):
        ahead, behind = ways(k)
        owned[k, 1].wait()
        ae[k, ahead].wait_recv()
        a2[k].wait_recv()
        for d in range(RING):
            bz[k, d].wait_recv()
        for j, (src, dst) in enumerate(((gk, gk_out), (gv, gv_out))):
            copy = pltpu.make_async_copy(src.at[k], dst.at[k], store.at[2 + 2 * k + j])
            copy.start()
            stores.append(copy)
        total = lax.dot_general(gk[k], wk[...], ACROSS, preferred_element_type=F32)
        total += lax.dot_general(gv[k], wv[...], ACROSS, preferred_element_type=F32)
        if k:
            fs[k] = total.astype(BF16)
            parts.append(
                go(fs.at[k], fr.at[SECTIONS - k], fx_s.at[k], fx_r.at[SECTIONS - k], along_x(k))
            )
        else:
            acc[...] = total

    def forward():
        turned = values[...].T
        for j in range(GROUP):
            out = jnp.dot(turned, probs[:, j * SEQ:(j + 1) * SEQ], preferred_element_type=F32)
            att[:, j * HD:(j + 1) * HD] = out.T.astype(BF16)
        copy = pltpu.make_async_copy(att, att_out, store.at[10])
        copy.start()
        stores.append(copy)

    n = len(TILES)
    for i in range(n + 3):
        if i < n:
            zero(TILES[i])
        if 0 <= i - 1 < n:
            one(TILES[i - 1])
        if i == n - 1:
            stores.append(turn(1))
        if i == n:
            forward()
        if 0 <= i - 2 < n:
            two(TILES[i - 2])
        if 0 <= i - 3:
            three(TILES[i - 3])
    for copy in parts:
        copy.wait_recv()
    total = acc[...]
    for k in (1, 2, 3):
        total = total + fr[k].astype(F32)
    fgrad[...] = total.astype(BF16)
    copy = pltpu.make_async_copy(fgrad, fgrad_out, store.at[11])
    copy.start()
    stores.append(copy)
    for copy in sends:
        copy.wait_send()
    for copy in stores:
        copy.wait()


def main(count, last, f, wk, wv, q, g):
    dma = pltpu.SemaphoreType.DMA
    vmem = pltpu.VMEM
    anywhere = pl.BlockSpec(memory_space=pl.ANY)
    rows = 4 * TILE
    wide = GROUP * SEQ
    return pl.pallas_call(
        main_kernel,
        out_shape=(
            jax.ShapeDtypeStruct((4, TILE, GROUP * HD), BF16),
            jax.ShapeDtypeStruct((4, TILE, GROUP * HD), BF16),
            jax.ShapeDtypeStruct((DEPTH, rows), BF16),
            jax.ShapeDtypeStruct((SEQ, GROUP * HD), BF16),
            jax.ShapeDtypeStruct((TILE, DEPTH), BF16),
        ),
        in_specs=[
            pl.BlockSpec(memory_space=pltpu.SMEM), pl.BlockSpec(memory_space=pltpu.VMEM),
        ] + [anywhere] * 5,
        out_specs=(anywhere,) * 5,
        scratch_shapes=[
            vmem((4, TILE, DEPTH), BF16),
            vmem((DEPTH, GROUP * HD), BF16),
            vmem((DEPTH, GROUP * HD), BF16),
            vmem((SEQ, GROUP * HD), BF16),
            vmem((SEQ, GROUP * HD), BF16),
            vmem((8, 8, HALF, HD), F32),
            vmem((8, 8, HALF, HD), F32),
            vmem((8, 4 * HALF + 16, HD), I16),
            vmem((8, 4 * HALF + 16, HD), I16),
            vmem((8, 4, HALF + 16, HD), I16),
            vmem((8, 4, HALF + 16, HD), I16),
            vmem((8, 4, 2, HALF, HD), BF16),
            vmem((8, 4, 2, HALF, HD), BF16),
            vmem((8, HALF, HD), BF16),
            vmem((8, HALF, HD), BF16),
            vmem((8, HALF, HD), F32),
            vmem((rows, HD), BF16),
            vmem((rows, HD), BF16),
            vmem((rows, wide), F32),
            vmem((rows, wide), F32),
            vmem((8, wide), F32),
            vmem((8, wide), F32),
            vmem((8, wide), F32),
            vmem((rows, wide), BF16),
            vmem((TILE, wide), BF16),
            vmem((4, TILE, HD), BF16),
            vmem((4, TILE, HD), BF16),
            vmem((4, TILE, GROUP * HD), BF16),
            vmem((4, TILE, GROUP * HD), BF16),
            vmem((4, TILE, DEPTH), BF16),
            vmem((4, TILE, DEPTH), BF16),
            vmem((TILE, DEPTH), F32),
            vmem((DEPTH, rows), BF16),
            vmem((SEQ, GROUP * HD), BF16),
            vmem((TILE, DEPTH), BF16),
            dma((5,)), dma((12,)), dma((4, 2)),
            dma((4, 2)), dma((4, 2)),
            dma((8,)), dma((8,)),
            dma((8, 4)), dma((8, 4)),
            dma((8, 4)), dma((8, 4)),
            dma((8,)), dma((8,)),
            dma((4,)), dma((4,)),
            dma((4, 4)), dma((4, 4)),
            dma((4,)), dma((4,)),
            dma((4, 4)), dma((4, 4)),
            dma((4,)), dma((4,)),
            dma((4, 4)), dma((4, 4)),
            dma((4,)), dma((4,)),
        ],
        compiler_params=pltpu.CompilerParams(
            collective_id=1, has_side_effects=True, vmem_limit_bytes=VMEM_LIMIT
        ),
        name="main",
    )(count, last, f, wk, wv, q, g)


def close_kernel(ft_ref, gk_ref, gv_ref, att_ref, fgrad_ref, kw_ref, vw_ref, att_out, fgrad_out):
    turned = ft_ref[...]
    kw_ref[...] = jnp.dot(turned, gk_ref[...], preferred_element_type=F32).astype(BF16)
    vw_ref[...] = jnp.dot(turned, gv_ref[...], preferred_element_type=F32).astype(BF16)
    att_out[...] = att_ref[...]
    fgrad_out[...] = fgrad_ref[...]


def close(ft, gk, gv, att, fgrad):
    step = 256

    def block(rows):
        return pl.BlockSpec((rows, step), lambda i: (0, i))

    rows = 4 * TILE
    return pl.pallas_call(
        close_kernel,
        grid=(DEPTH // step,),
        out_shape=(
            jax.ShapeDtypeStruct((DEPTH, GROUP * HD), BF16),
            jax.ShapeDtypeStruct((DEPTH, GROUP * HD), BF16),
            jax.ShapeDtypeStruct((SEQ, GROUP * HD), BF16),
            jax.ShapeDtypeStruct((TILE, DEPTH), BF16),
        ),
        in_specs=[
            pl.BlockSpec((DEPTH, rows), lambda i: (0, 0)),
            block(rows), block(rows), block(SEQ), block(TILE),
        ],
        out_specs=(block(DEPTH), block(DEPTH), block(SEQ), block(TILE)),
        compiler_params=pltpu.CompilerParams(vmem_limit_bytes=VMEM_LIMIT),
        name="close",
    )(ft, gk, gv, att, fgrad)


def per_device(features, key_weight, value_weight, queries, out_grad, tile_count, tile_last):
    gk, gv, ft, att, fgrad = main(
        tile_count, tile_last.reshape(1, SEQ), features,
        key_weight[0], value_weight[0], queries[0], out_grad[0],
    )
    rows = 4 * TILE
    kgrad, vgrad, out, fgrad = close(
        ft, gk.reshape(rows, GROUP * HD), gv.reshape(rows, GROUP * HD), att, fgrad
    )
    return (out[None], fgrad, kgrad[None], vgrad[None])


def solution(mesh):
    in_specs = (
        P(("dp", "section"), "tensor"),
        P("section", "tensor", None),
        P("section", "tensor", None),
        P("section", "dp", "tensor"),
        P("section", "dp", "tensor"),
        P("dp"),
        P("dp"),
    )
    out_specs = (
        P("section", "dp", "tensor"),
        P(("dp", "section"), "tensor"),
        P("section", "tensor", "dp"),
        P("section", "tensor", "dp"),
    )
    return jax.shard_map(
        per_device, mesh=mesh, in_specs=in_specs, out_specs=out_specs, check_vma=False
    )
```

time: 349 us -> 83.5 us (0.24)
  waiting for transfers between devices: 268 us -> 0 us
  Pallas kernels: 0 us -> 81.7 us
  matrix products: 42.9 us -> 0 us
  local copies, waits for them, and re-layouts: 13.7 us -> 0 us
  between operations: 13.9 us -> 0.78 us
  other arithmetic: 8.03 us -> 0 us
    reduce_scatter x2 -> x0, waiting for transfers between devices: 148 us -> none  [the longest x1 129 us: per_device(): lax.psum_scatter(partial_sums, 'tensor', scatter_dimension=2, tiled=True)]
    all_gather x3 -> x0, waiting for transfers between devices: 119 us -> none  [the longest x1 45.8 us: per_device(): lax.all_gather(dkeys, 'tensor', axis=1, tiled=True)]
    pallas_call x0 -> x2, Pallas kernels: none -> 81.7 us  [the longest x1 74.2 us: main(): pl.pallas_call(main_kernel, out_shape=(jax.ShapeDtypeStruct((4, TILE, GRO...]
    dot_general x11 -> x0, matrix products: 42.9 us -> none  [the longest x1 6.53 us: per_device(): lax.dot_general(dkeys_all, key_w, contract_cols, preferred_element_type=j...]
    unnamed x19 -> x0, local copies, waits for them, and re-layouts: 13.7 us -> none
  transfers between devices with their start and end apart: 5 -> 0, of which waited for: 5 -> 0; matrix products, arithmetic and copies ran while one was open for 11% -> 0% of each run, Pallas kernels for 0% -> 0%
where the time goes in v2:
time: 83.5 us; the launch traced here: 82.5 us
  Pallas kernels  81.7 us (98%)
    pallas_call x1, Pallas kernels, main(): pl.pallas_call(main_kernel, out_shape=(jax.ShapeDtypeStruct((4, TILE, GRO...  74.2 us
    pallas_call x1, Pallas kernels, close(): pl.pallas_call(close_kernel, grid=(DEPTH // step,), out_shape=(jax.ShapeD...  7.59 us

profile of v2, /device:TPU:64, one launch (start us, length us, event | category | flops | bytes accessed | tf_op | source)
XLA Modules:
  0.0 82.5 jit_solution(3017501548159719837)
XLA Ops:
  0.6 74.2 %main.1 = (bf16[4,192,1024]{2,1,0:T(8,128)(2,1)}, bf16[4,192,1024]{2,1,0:T(8,128)(2,1)}, bf16[1024,768]{1,0:T(8,128)(2,1)}, bf16[256,1024]{1,0:T(8,128)(2,1)}, bf16[192,1024]{1,0:T(8,128)(2,1)}) custom-call(s32[4]{0:T(128)} %count_ref.1, s32[1,256]{1,0:T(1,128)} %bitcast.16, bf16[192,1024]{1,0:T(8,128)(2,1)} %f_ref.1, bf16[1024,1024]{1,0:T(8,128)(2,1)} %bitcast.10, ...), custom_call_target="tpu_custom_call" | custom-call | tf_op jit(solution)/shard_map/main/pallas_call | solution.py:392
  74.8 7.6 %close.1 = (bf16[1024,1024]{1,0:T(8,128)(2,1)}, bf16[1024,1024]{1,0:T(8,128)(2,1)}, bf16[256,1024]{1,0:T(8,128)(2,1)}, bf16[192,1024]{1,0:T(8,128)(2,1)}) custom-call(bf16[1024,768]{1,0:T(8,128)(2,1)} %get-tuple-element.13.ft_ref, bf16[768,1024]{1,0:T(8,128)(2,1)} %bitcast.12, bf16[768,1024]{1,0:T(8,128)(2,1)} %bitcast.13, ...), custom_call_target="tpu_custom_call" | custom-call | tf_op jit(solution)/shard_map/close/pallas_call | solution.py:477

commit v3 on v2

v3 whole, which is shorter than its diff:
```python
import functools

import jax
import jax.numpy as jnp
from jax import lax
from jax.experimental import pallas as pl
from jax.experimental.pallas import tpu as pltpu
from jax.sharding import PartitionSpec as P

MESH = pl.DeviceIdType.MESH
F32 = jnp.float32
BF16 = jnp.bfloat16
I16 = jnp.int16
HD = 128
GROUP = 8
SECTIONS = 4
RING = 4
TILE = 192
HALF = TILE // 2
DEPTH = 1024
SEQ = 256
LEVELS = 32700.0
FLOOR = -1e30
VMEM_LIMIT = 58 * 2**20


def place():
    t = lax.axis_index("tensor")
    return lax.axis_index("section"), lax.axis_index("dp"), t // 2, lax.rem(t, 2)


def along_x(d):
    s, dp, y, z = place()
    return (lax.rem(s + d, SECTIONS), dp, y * 2 + z)


def along_y(d):
    s, dp, y, z = place()
    return (s, dp, lax.rem(y + d, RING) * 2 + z)


def along_z():
    s, dp, y, z = place()
    return (s, dp, y * 2 + (1 - z))


def greet():
    barrier = pltpu.get_barrier_semaphore()
    peers = [along_x(d) for d in (1, 3)] + [along_y(d) for d in (1, 2, 3)] + [along_z()]
    for peer in peers:
        pl.semaphore_signal(barrier, inc=1, device_id=peer, device_id_type=MESH)
    return barrier, len(peers)


def remote(src, dst, send_sem, recv_sem, device):
    return pltpu.make_async_remote_copy(
        src_ref=src, dst_ref=dst, send_sem=send_sem, recv_sem=recv_sem,
        device_id=device, device_id_type=MESH,
    )


def encode(x):
    top = jnp.maximum(jnp.max(jnp.abs(x), axis=0, keepdims=True), 1e-30)
    power = jnp.ceil(jnp.log(top) * 1.4426950408889634 + 0.0005)
    code = jnp.round(x * (jnp.exp2(-power) * LEVELS)).astype(jnp.int32).astype(I16)
    return code, power


def marks(powers):
    row = lax.broadcasted_iota(jnp.int32, (16, HD), 0)
    mark = jnp.broadcast_to(powers[0], (16, HD))
    for i, power in enumerate(powers[1:]):
        mark = jnp.where(row == i + 1, power, mark)
    return mark.astype(jnp.int32).astype(I16)


def units(mark):
    return jnp.exp2(mark.astype(jnp.int32).astype(F32)) * (1.0 / LEVELS)


def as_f32(code):
    return code.astype(jnp.int32).astype(F32)


ACROSS = (((1,), (1,)), ((), ()))
CHUNKS = ((0, 0), (0, 1), (1, 0), (3, 0), (1, 1), (3, 1), (2, 0), (2, 1))
UNITS = (((2, 0), (2, 1)), ((1, 0), (3, 0)), ((1, 1), (3, 1)), ((0, 0), (0, 1)))
ROWS = sum(UNITS, ())
RELAYED = 6
SLOT = {1: 0, 3: 1, 2: 2}


def ahead_of(i):
    return 1 if i % 2 == 0 else 3


def main_kernel(
    count_hbm, last_hbm, f_ref, wk_ref, wv_ref, q_ref, g_ref,
    kgrad, vgrad, att, fgrad,
    fg, wk, wv, q, g, pk, pv, kz_out, kz_in, ky_out, ky_in, vy_out, vy_in, vz_out, vz_in, sv,
    keys, values, expo, dprobs, tops, sums, dots, probs, dscores, dks, dvs, gk, gv, fs, fr, acc,
    ft, count, last,
    load, out1, out3, x_out, x_in, kz_sem, v1_sem, v2_sem, k1_sem, k2_sem, vz_sem,
    a1_sem, a2_sem, a3_sem, over_sem, part_sem,
):
    s, dp, y, z = place()
    scale = HD ** -0.5
    loads = [
        pltpu.make_async_copy(src, dst, load.at[i])
        for i, (src, dst) in enumerate((
            (f_ref, fg.at[0]), (wv_ref, wv), (wk_ref, wk), (q_ref, q), (g_ref, g),
            (last_hbm, last), (count_hbm, count),
        ))
    ]
    for copy in loads:
        copy.start()
    barrier, peers = greet()

    def go(*args):
        remote(*args).start()

    def done(ref, sem):
        pltpu.make_async_copy(ref, ref, sem).wait()

    def half(k, h):
        return fg.at[k, pl.ds(h * HALF, HALF)]

    def pass_x(k, h, to, d, sem):
        go(half(k, h), half(to, h), sem, x_in.at[to - 1, h], along_x(d))

    def head_at(d, r):
        return lax.rem(y + d, RING) * 2 + lax.rem(z + r, 2)

    def compute_v(i):
        k, h = CHUNKS[i]
        v = jnp.dot(fg[k, h * HALF:(h + 1) * HALF, :], wv[...], preferred_element_type=F32)
        for head in range(8):
            pv[i, head] = v[:, head * HD:(head + 1) * HD]
        for d in (2, RING - ahead_of(i)) if i < RELAYED else (2, 1, 3):
            for r in range(2):
                vy_out[i, SLOT[d], r] = pv[i, head_at(d, r)].astype(BF16)

    def compute_k(i):
        k, h = CHUNKS[i]
        p = jnp.dot(fg[k, h * HALF:(h + 1) * HALF, :], wk[...], preferred_element_type=F32)
        for head in range(8):
            pk[i, head] = p[:, head * HD:(head + 1) * HD]
        powers = []
        for d in range(RING):
            code, power = encode(pk[i, head_at(d, 1)])
            kz_out[i, d * HALF:(d + 1) * HALF, :] = code
            powers.append(power)
        kz_out[i, 4 * HALF:4 * HALF + 16, :] = marks(powers)

    def send_y(i, d, to, at, sem):
        go(vy_out.at[i, SLOT[d]], vy_in.at[i, SLOT[at]], out1, sem.at[i], along_y(to))

    def send_v(i):
        ahead = ahead_of(i)
        if i < RELAYED:
            send_y(i, 2, ahead, 2, v1_sem)
            send_y(i, RING - ahead, RING - ahead, ahead, v2_sem)
        else:
            for d in (2, 1, 3):
                send_y(i, d, d, RING - d, v1_sem)

    def send_z(i):
        go(kz_out.at[i], kz_in.at[i], out1, kz_sem.at[i], along_z())

    def start(i):
        k, h = CHUNKS[i]
        if k == 2:
            done(half(k, h), x_in.at[k - 1, h])
        compute_v(i)
        send_v(i)
        compute_k(i)
        send_z(i)

    def send_k(i, d, to, at, total, sem):
        code, power = encode(total)
        ky_out[i, SLOT[d], 0:HALF, :] = code
        ky_out[i, SLOT[d], HALF:HALF + 16, :] = marks([power])
        go(ky_out.at[i, SLOT[d]], ky_in.at[i, SLOT[at]], out1, sem.at[i], along_y(to))

    def got_k(i, at):
        unit = units(ky_in[i, at, HALF:HALF + 16, :])
        return as_f32(ky_in[i, at, 0:HALF, :]) * unit[0:1]

    def gather_v(i, n, sem):
        done(vy_in.at[i, pl.ds(0, n)], sem.at[i])
        for r in (1, 0):
            total = pv[i, head_at(0, r)]
            for at in range(n):
                total = total + vy_in[i, at, r].astype(F32)
            if r:
                vz_out[i] = total.astype(BF16)
                go(vz_out.at[i], vz_in.at[i], out1, vz_sem.at[i], along_z())
            else:
                sv[i] = total

    def middle(i):
        ahead = ahead_of(i)
        behind = RING - ahead
        if i < RELAYED:
            done(vy_in.at[i, 2], v1_sem.at[i])
            for r in range(2):
                total = pv[i, head_at(ahead, r)] + vy_in[i, 2, r].astype(F32)
                vy_out[i, SLOT[ahead], r] = total.astype(BF16)
            send_y(i, ahead, ahead, behind, v2_sem)
        done(kz_in.at[i], kz_sem.at[i])
        unit = units(kz_in[i, 4 * HALF:4 * HALF + 16, :])
        for d in (2, 1, 3, 0):
            head = head_at(d, 0)
            total = pk[i, head] + as_f32(kz_in[i, d * HALF:(d + 1) * HALF, :]) * unit[d:d + 1]
            if i >= RELAYED and d:
                send_k(i, d, d, RING - d, total, k2_sem)
            elif d == 2:
                send_k(i, 2, behind, 2, total, k1_sem)
            elif d == ahead:
                send_k(i, ahead, ahead, behind, total, k2_sem)
            else:
                pk[i, head] = total
        if i >= RELAYED:
            gather_v(i, 3, v1_sem)

    def relay(i):
        ahead = ahead_of(i)
        behind = RING - ahead
        done(ky_in.at[i, 2], k1_sem.at[i])
        send_k(i, behind, behind, ahead, pk[i, head_at(behind, 0)] + got_k(i, 2), k2_sem)
        gather_v(i, 2, v2_sem)

    def finish(i):
        k, h = CHUNKS[i]
        at = ROWS.index((k, h)) * HALF
        spot = slice(at, at + HALF)
        n = 2 if i < RELAYED else 3
        done(ky_in.at[i, pl.ds(0, n)], k2_sem.at[i])
        total = pk[i, head_at(0, 0)]
        for at in range(n):
            total = total + got_k(i, at)
        key = total.astype(BF16)
        keys[spot, :] = key
        done(vz_in.at[i], vz_sem.at[i])
        value = (sv[i] + vz_in[i].astype(F32)).astype(BF16)
        values[spot, :] = value
        tile = lax.rem(s + k, SECTIONS)
        slot = lax.broadcasted_iota(jnp.int32, (HALF, SEQ), 0) + h * HALF
        limit = jnp.where(slot < count[tile], tile, SECTIONS)
        visible = limit <= last[...]
        for j in range(GROUP):
            cols = slice(j * HD, (j + 1) * HD)
            wide = slice(j * SEQ, (j + 1) * SEQ)
            scores = lax.dot_general(key, q[:, cols], ACROSS, preferred_element_type=F32) * scale
            masked = jnp.where(visible, scores, -jnp.inf)
            top = jnp.maximum(jnp.max(masked, axis=0, keepdims=True), FLOOR)
            e = jnp.exp(masked - top)
            dprob = lax.dot_general(value, g[:, cols], ACROSS, preferred_element_type=F32)
            expo[spot, wide] = e
            dprobs[spot, wide] = dprob
            tops[i:i + 1, wide] = top
            sums[i:i + 1, wide] = jnp.sum(e, axis=0, keepdims=True)
            dots[i:i + 1, wide] = jnp.sum(e * dprob, axis=0, keepdims=True)

    def turn(a):
        rows = [fg[k, h * HALF:(h + 1) * HALF, :] for k, h in ROWS[4 * a:4 * a + 4]]
        ft[:, a * 2 * TILE:(a + 1) * 2 * TILE] = jnp.concatenate(rows, axis=0).T

    loads[0].wait()
    loads[1].wait()
    compute_v(0)
    pl.semaphore_wait(barrier, peers)
    pass_x(0, 0, 3, 1, x_out)
    pass_x(0, 0, 1, 3, x_out)
    send_v(0)
    loads[2].wait()
    compute_k(0)
    send_z(0)
    start(1)
    middle(0)
    done(fg.at[0], x_out)
    pass_x(0, 1, 3, 1, out1)
    pass_x(0, 1, 1, 3, out1)
    middle(1)
    done(half(1, 0), x_in.at[0, 0])
    pass_x(1, 0, 2, 3, out1)
    start(2)
    done(half(3, 0), x_in.at[2, 0])
    start(3)
    for copy in loads[3:]:
        copy.wait()
    relay(0)
    relay(1)
    done(half(3, 1), x_in.at[2, 1])
    pass_x(3, 1, 2, 1, out1)
    done(half(1, 1), x_in.at[0, 1])
    start(4)
    middle(2)
    finish(0)
    start(5)
    middle(3)
    finish(1)
    relay(2)
    start(6)
    middle(4)
    relay(3)
    finish(2)
    start(7)
    middle(5)
    relay(4)
    finish(3)
    middle(6)
    relay(5)
    finish(4)
    turn(0)
    turn(1)
    middle(7)
    finish(5)
    finish(6)
    finish(7)

    peak = jnp.max(tops[...], axis=0, keepdims=True)
    share = jnp.exp(tops[...] - peak)
    inverse = 1.0 / jnp.sum(share * sums[...], axis=0, keepdims=True)
    share = share * inverse
    sums[...] = share
    dots[0:1, :] = jnp.sum(share * dots[...], axis=0, keepdims=True)

    def cols(head, n=1):
        return pl.ds(pl.multiple_of(head * HD, HD), n * HD)

    mine = cols(y * 2 + z)

    def attend(k):
        dk = dv = None
        for j in range(GROUP):
            narrow = slice(j * HD, (j + 1) * HD)
            wide = slice(j * SEQ, (j + 1) * SEQ)
            delta = dots[0:1, wide]
            for h in range(2):
                i = CHUNKS.index(UNITS[k][h])
                spot = slice(k * TILE + h * HALF, k * TILE + (h + 1) * HALF)
                p = expo[spot, wide] * sums[i:i + 1, wide]
                probs[spot, wide] = p.astype(BF16)
                dscores[h * HALF:(h + 1) * HALF, wide] = (p * (dprobs[spot, wide] - delta) * scale).astype(BF16)
            whole = slice(k * TILE, (k + 1) * TILE)
            dv_j = jnp.dot(probs[whole, wide], g[:, narrow], preferred_element_type=F32)
            dk_j = jnp.dot(dscores[:, wide], q[:, narrow], preferred_element_type=F32)
            dv = dv_j if j == 0 else dv + dv_j
            dk = dk_j if j == 0 else dk + dk_j
        for ref, into, value in ((dvs, gv, dv), (dks, gk, dk)):
            rounded = value.astype(BF16)
            ref[k] = rounded
            into[k, :, mine] = rounded

    def ways(k):
        return (1, 3) if k % 2 == 0 else (3, 1)

    def zero(k):
        go(dvs.at[k], gv.at[k, :, mine], out3, a1_sem.at[k], along_y(1))
        go(dvs.at[k], gv.at[k, :, mine], out3, a1_sem.at[k], along_y(3))
        go(dks.at[k], gk.at[k, :, mine], out3, a1_sem.at[k], along_z())
        go(dvs.at[k], gv.at[k, :, mine], out3, a3_sem.at[k], along_z())

    def one(k):
        ahead, behind = ways(k)
        done(gk.at[k, :, pl.ds(0, 3 * HD)], a1_sem.at[k])
        pair = cols(y * 2, 2)
        go(gk.at[k, :, pair], gk.at[k, :, pair], out3, a2_sem.at[k], along_y(ahead))
        head = cols(head_at(behind, 0))
        go(gv.at[k, :, head], gv.at[k, :, head], out3, a2_sem.at[k], along_y(ahead))
        go(gk.at[k, :, pair], gk.at[k, :, pair], out3, a3_sem.at[k], along_y(behind))
        for d in (behind, ahead):
            head = cols(head_at(d, 0))
            go(gv.at[k, :, head], gv.at[k, :, head], out3, a3_sem.at[k], along_z())

    def two(k):
        ahead, behind = ways(k)
        done(gk.at[k, :, pl.ds(0, 3 * HD)], a2_sem.at[k])
        pair = cols(lax.rem(y + behind, RING) * 2, 2)
        go(gk.at[k, :, pair], gk.at[k, :, pair], out3, a3_sem.at[k], along_y(ahead))
        head = cols(head_at(2, 0))
        go(gv.at[k, :, head], gv.at[k, :, head], out3, a3_sem.at[k], along_z())

    def three(k):
        done(gk.at[k], a3_sem.at[k])
        total = lax.dot_general(gk[k], wk[...], ACROSS, preferred_element_type=F32)
        total += lax.dot_general(gv[k], wv[...], ACROSS, preferred_element_type=F32)
        for h, (tile, part) in enumerate(UNITS[k]):
            half_total = total[h * HALF:(h + 1) * HALF]
            if tile == 0:
                acc[h * HALF:(h + 1) * HALF, :] = half_total
                continue
            way = tile if tile != 2 else (3, 1)[part]
            if (tile, part) in ((1, 1), (3, 0)):
                done(fr.at[2, part], over_sem.at[part])
                half_total = half_total + fr[2, part].astype(F32)
            fs[tile, part] = half_total.astype(BF16)
            if tile == 2:
                go(fs.at[tile, part], fr.at[2, part], out3, over_sem.at[part], along_x(way))
            else:
                go(fs.at[tile, part], fr.at[SLOT[SECTIONS - way], part], out3, part_sem, along_x(way))

    def weights(a, j):
        rows = slice(a * 2 * TILE, (a + 1) * 2 * TILE)
        side = slice(j * DEPTH, (j + 1) * DEPTH)
        src, dst = ((gk, kgrad), (gv, vgrad))[j]
        rhs = jnp.concatenate([src[2 * a], src[2 * a + 1]], axis=0)
        total = jnp.dot(ft[:, rows], rhs, preferred_element_type=F32)
        if a == 0:
            expo[0:3 * SEQ, side] = total[0:3 * SEQ]
            dprobs[0:SEQ, side] = total[3 * SEQ:4 * SEQ]
        else:
            dst[0:3 * SEQ, :] = (expo[0:3 * SEQ, side] + total[0:3 * SEQ]).astype(BF16)
            dst[3 * SEQ:4 * SEQ, :] = (dprobs[0:SEQ, side] + total[3 * SEQ:4 * SEQ]).astype(BF16)

    def forward():
        turned = values[...].T
        for j in range(GROUP):
            out = jnp.dot(turned, probs[:, j * SEQ:(j + 1) * SEQ], preferred_element_type=F32)
            att[:, j * HD:(j + 1) * HD] = out.T.astype(BF16)

    attend(0)
    zero(0)
    attend(1)
    zero(1)
    one(0)
    attend(2)
    zero(2)
    one(1)
    two(0)
    attend(3)
    zero(3)
    one(2)
    two(1)
    three(0)
    one(3)
    forward()
    two(2)
    three(1)
    two(3)
    weights(0, 0)
    three(2)
    weights(0, 1)
    three(3)
    weights(1, 0)
    weights(1, 1)
    done(fr.at[pl.ds(0, 2)], part_sem)
    for h in range(2):
        rows = slice(h * HALF, (h + 1) * HALF)
        total = acc[rows, :]
        for at in (0, 1):
            total = total + fr[at, h].astype(F32)
        fgrad[rows, :] = total.astype(BF16)
    done(expo.at[pl.ds(0, 448)], out1)
    done(expo.at[pl.ds(0, 480)], out3)


def main(count, last, f, wk, wv, q, g):
    dma = pltpu.SemaphoreType.DMA
    vmem = pltpu.VMEM
    held = pl.BlockSpec(memory_space=pltpu.HBM)
    rows = 4 * TILE
    wide = GROUP * SEQ
    return pl.pallas_call(
        main_kernel,
        out_shape=(
            vmem((DEPTH, GROUP * HD), BF16),
            vmem((DEPTH, GROUP * HD), BF16),
            vmem((SEQ, GROUP * HD), BF16),
            vmem((TILE, DEPTH), BF16),
        ),
        in_specs=[held] * 7,
        out_specs=(pl.BlockSpec(memory_space=pltpu.VMEM),) * 4,
        scratch_shapes=[
            vmem((4, TILE, DEPTH), BF16),
            vmem((DEPTH, GROUP * HD), BF16),
            vmem((DEPTH, GROUP * HD), BF16),
            vmem((SEQ, GROUP * HD), BF16),
            vmem((SEQ, GROUP * HD), BF16),
            vmem((8, 8, HALF, HD), F32),
            vmem((8, 8, HALF, HD), F32),
            vmem((8, 4 * HALF + 16, HD), I16),
            vmem((8, 4 * HALF + 16, HD), I16),
            vmem((8, 3, HALF + 16, HD), I16),
            vmem((8, 3, HALF + 16, HD), I16),
            vmem((8, 3, 2, HALF, HD), BF16),
            vmem((8, 3, 2, HALF, HD), BF16),
            vmem((8, HALF, HD), BF16),
            vmem((8, HALF, HD), BF16),
            vmem((8, HALF, HD), F32),
            vmem((rows, HD), BF16),
            vmem((rows, HD), BF16),
            vmem((rows, wide), F32),
            vmem((rows, wide), F32),
            vmem((8, wide), F32),
            vmem((8, wide), F32),
            vmem((8, wide), F32),
            vmem((rows, wide), BF16),
            vmem((TILE, wide), BF16),
            vmem((4, TILE, HD), BF16),
            vmem((4, TILE, HD), BF16),
            vmem((4, TILE, GROUP * HD), BF16),
            vmem((4, TILE, GROUP * HD), BF16),
            vmem((4, 2, HALF, DEPTH), BF16),
            vmem((4, 2, HALF, DEPTH), BF16),
            vmem((TILE, DEPTH), F32),
            vmem((DEPTH, rows), BF16),
            pltpu.SMEM((4,), jnp.int32),
            vmem((1, SEQ), jnp.int32),
            dma((7,)), dma, dma, dma, dma((3, 2)),
            dma((8,)), dma((8,)), dma((6,)), dma((6,)), dma((8,)), dma((8,)),
            dma((4,)), dma((4,)), dma((4,)), dma((2,)), dma,
        ],
        compiler_params=pltpu.CompilerParams(
            collective_id=1, has_side_effects=True, vmem_limit_bytes=VMEM_LIMIT
        ),
        name="main",
    )(count, last, f, wk, wv, q, g)


PIECES = 2


def close_kernel(*refs):
    n = 4
    ins, outs, done = refs[:n], refs[n:2 * n], refs[2 * n]
    copies = []
    for i in range(n):
        rows = ins[i].shape[0] // PIECES
        for j in range(PIECES):
            part = pl.ds(j * rows, rows)
            copies.append(pltpu.make_async_copy(ins[i].at[part], outs[i].at[part], done.at[i, j]))
    for copy in copies:
        copy.start()
    for copy in copies:
        copy.wait()


def close(*arrays):
    n = len(arrays)
    return pl.pallas_call(
        close_kernel,
        out_shape=tuple(jax.ShapeDtypeStruct(x.shape, x.dtype) for x in arrays),
        in_specs=[pl.BlockSpec(memory_space=pltpu.VMEM)] * n,
        out_specs=(pl.BlockSpec(memory_space=pltpu.HBM),) * n,
        scratch_shapes=[pltpu.SemaphoreType.DMA((n, PIECES))],
        compiler_params=pltpu.CompilerParams(vmem_limit_bytes=8 * 2**20),
        name="close",
    )(*arrays)


def per_device(features, key_weight, value_weight, queries, out_grad, tile_count, tile_last):
    kgrad, vgrad, out, fgrad = close(*main(
        tile_count, tile_last.reshape(1, SEQ), features,
        key_weight[0], value_weight[0], queries[0], out_grad[0],
    ))
    return (out[None], fgrad, kgrad[None], vgrad[None])


def solution(mesh):
    in_specs = (
        P(("dp", "section"), "tensor"),
        P("section", "tensor", None),
        P("section", "tensor", None),
        P("section", "dp", "tensor"),
        P("section", "dp", "tensor"),
        P("dp"),
        P("dp"),
    )
    out_specs = (
        P("section", "dp", "tensor"),
        P(("dp", "section"), "tensor"),
        P("section", "tensor", "dp"),
        P("section", "tensor", "dp"),
    )
    return jax.shard_map(
        per_device, mesh=mesh, in_specs=in_specs, out_specs=out_specs, check_vma=False
    )
```

time: 83.5 us -> 73.2 us (0.88); the launches traced: 82.5 us -> 73.1 us
  Pallas kernels: 81.7 us -> 72.3 us
    pallas_call x2, Pallas kernels: 81.7 us -> 72.3 us  [the longest x1 70 us: main(): pl.pallas_call(main_kernel, out_shape=(vmem((DEPTH, GROUP * HD), BF16), v...]
where the time goes in v3:
time: 73.2 us; the launch traced here: 73.1 us
  Pallas kernels  72.3 us (99%)
  between operations  0.8 us (1%)
    pallas_call x1, Pallas kernels, main(): pl.pallas_call(main_kernel, out_shape=(vmem((DEPTH, GROUP * HD), BF16), v...  70 us
    pallas_call x1, Pallas kernels, close(): pl.pallas_call(close_kernel, out_shape=tuple((jax.ShapeDtypeStruct(x.shap...  2.35 us

profile of v3, /device:TPU:64, one launch (start us, length us, event | category | flops | bytes accessed | tf_op | source)
XLA Modules:
  0.0 73.1 jit_solution(17529524906814338459)
XLA Ops:
  0.6 70.0 %main.1 = (bf16[1024,1024]{1,0:T(8,128)(2,1)S(1)}, bf16[1024,1024]{1,0:T(8,128)(2,1)S(1)}, bf16[256,1024]{1,0:T(8,128)(2,1)S(1)}, bf16[192,1024]{1,0:T(8,128)(2,1)S(1)}) custom-call(s32[4]{0:T(128)} %count_hbm.1, s32[1,256]{1,0:T(1,128)} %bitcast.12, bf16[192,1024]{1,0:T(8,128)(2,1)} %f_ref.1, bf16[1024,1024]{1,0:T(8,128)(2,1)} %bitcast.8, ...), custom_call_target="tpu_custom_call" | custom-call | tf_op jit(solution)/shard_map/main/pallas_call | solution.py:465
  70.6 2.3 %close.1 = (bf16[1024,1024]{1,0:T(8,128)(2,1)}, bf16[1024,1024]{1,0:T(8,128)(2,1)}, bf16[256,1024]{1,0:T(8,128)(2,1)}, bf16[192,1024]{1,0:T(8,128)(2,1)}) custom-call(bf16[1024,1024]{1,0:T(8,128)(2,1)S(1)} %get-tuple-element.12.refs_0_, bf16[1024,1024]{1,0:T(8,128)(2,1)S(1)} %get-tuple-element.13.refs_1_, bf16[256,1024]{1,0:T(8,128)(2,1)S(1)} %get-tuple-element.14.refs_2_, ...), custom_call_target="tpu_custom_call" | custom-call | tf_op jit(solution)/shard_map/close/pallas_call | solution.py:542

commit v4 on v3

--- a/solution.py
+++ b/solution.py
@@ -101,7 +101,7 @@
     keys, values, expo, dprobs, tops, sums, dots, probs, dscores, dks, dvs, gk, gv, fs, fr, acc,
     ft, count, last,
     load, out1, out3, x_out, x_in, kz_sem, v1_sem, v2_sem, k1_sem, k2_sem, vz_sem,
-    a1_sem, a2_sem, a3_sem, over_sem, part_sem,
+    az_sem, by_sem, b2_sem, a2_sem, a3_sem, over_sem, part_sem,
 ):
     s, dp, y, z = place()
     scale = HD ** -0.5
@@ -283,38 +283,38 @@
     pass_x(0, 1, 1, 3, out1)
     middle(1)
     done(half(1, 0), x_in.at[0, 0])
-    pass_x(1, 0, 2, 3, out1)
     start(2)
     done(half(3, 0), x_in.at[2, 0])
     start(3)
+    relay(0)
+    relay(1)
     for copy in loads[3:]:
         copy.wait()
-    relay(0)
-    relay(1)
+    done(half(1, 1), x_in.at[0, 1])
+    pass_x(1, 0, 2, 3, out1)
     done(half(3, 1), x_in.at[2, 1])
     pass_x(3, 1, 2, 1, out1)
-    done(half(1, 1), x_in.at[0, 1])
     start(4)
     middle(2)
-    finish(0)
     start(5)
     middle(3)
+    relay(2)
+    finish(0)
     finish(1)
-    relay(2)
     start(6)
     middle(4)
     relay(3)
-    finish(2)
     start(7)
     middle(5)
     relay(4)
-    finish(3)
+    finish(2)
     middle(6)
     relay(5)
+    finish(3)
+    middle(7)
     finish(4)
     turn(0)
     turn(1)
-    middle(7)
     finish(5)
     finish(6)
     finish(7)
@@ -326,10 +326,10 @@
     sums[...] = share
     dots[0:1, :] = jnp.sum(share * dots[...], axis=0, keepdims=True)
 
-    def cols(head, n=1):
-        return pl.ds(pl.multiple_of(head * HD, HD), n * HD)
-
-    mine = cols(y * 2 + z)
+    mine = y * 2 + z
+
+    def heads(ref, k):
+        return jnp.concatenate([ref[k, head] for head in range(8)], axis=1)
 
     def attend(k):
         dk = dv = None
@@ -351,41 +351,43 @@
         for ref, into, value in ((dvs, gv, dv), (dks, gk, dk)):
             rounded = value.astype(BF16)
             ref[k] = rounded
-            into[k, :, mine] = rounded
+            into[k, mine] = rounded
 
     def ways(k):
         return (1, 3) if k % 2 == 0 else (3, 1)
 
     def zero(k):
-        go(dvs.at[k], gv.at[k, :, mine], out3, a1_sem.at[k], along_y(1))
-        go(dvs.at[k], gv.at[k, :, mine], out3, a1_sem.at[k], along_y(3))
-        go(dks.at[k], gk.at[k, :, mine], out3, a1_sem.at[k], along_z())
-        go(dvs.at[k], gv.at[k, :, mine], out3, a3_sem.at[k], along_z())
+        for d in (1, 3):
+            go(dvs.at[k], gv.at[k, mine], out3, by_sem.at[k, SLOT[RING - d]], along_y(d))
+        go(dks.at[k], gk.at[k, mine], out3, az_sem.at[k], along_z())
+        go(dvs.at[k], gv.at[k, mine], out3, a3_sem.at[k], along_z())
 
     def one(k):
         ahead, behind = ways(k)
-        done(gk.at[k, :, pl.ds(0, 3 * HD)], a1_sem.at[k])
-        pair = cols(y * 2, 2)
-        go(gk.at[k, :, pair], gk.at[k, :, pair], out3, a2_sem.at[k], along_y(ahead))
-        head = cols(head_at(behind, 0))
-        go(gv.at[k, :, head], gv.at[k, :, head], out3, a2_sem.at[k], along_y(ahead))
-        go(gk.at[k, :, pair], gk.at[k, :, pair], out3, a3_sem.at[k], along_y(behind))
+        done(gk.at[k, 0], az_sem.at[k])
+        pair = pl.ds(y * 2, 2)
+        go(gk.at[k, pair], gk.at[k, pair], out3, a2_sem.at[k], along_y(ahead))
+        go(gk.at[k, pair], gk.at[k, pair], out3, a3_sem.at[k], along_y(behind))
         for d in (behind, ahead):
-            head = cols(head_at(d, 0))
-            go(gv.at[k, :, head], gv.at[k, :, head], out3, a3_sem.at[k], along_z())
+            done(gv.at[k, 0], by_sem.at[k, SLOT[d]])
+            head = head_at(d, 0)
+            if d == behind:
+                go(gv.at[k, head], gv.at[k, head], out3, b2_sem.at[k], along_y(ahead))
+            go(gv.at[k, head], gv.at[k, head], out3, a3_sem.at[k], along_z())
 
     def two(k):
         ahead, behind = ways(k)
-        done(gk.at[k, :, pl.ds(0, 3 * HD)], a2_sem.at[k])
-        pair = cols(lax.rem(y + behind, RING) * 2, 2)
-        go(gk.at[k, :, pair], gk.at[k, :, pair], out3, a3_sem.at[k], along_y(ahead))
-        head = cols(head_at(2, 0))
-        go(gv.at[k, :, head], gv.at[k, :, head], out3, a3_sem.at[k], along_z())
+        done(gk.at[k, pl.ds(0, 2)], a2_sem.at[k])
+        pair = pl.ds(lax.rem(y + behind, RING) * 2, 2)
+        go(gk.at[k, pair], gk.at[k, pair], out3, a3_sem.at[k], along_y(ahead))
+        done(gv.at[k, 0], b2_sem.at[k])
+        head = head_at(2, 0)
+        go(gv.at[k, head], gv.at[k, head], out3, a3_sem.at[k], along_z())
 
     def three(k):
         done(gk.at[k], a3_sem.at[k])
-        total = lax.dot_general(gk[k], wk[...], ACROSS, preferred_element_type=F32)
-        total += lax.dot_general(gv[k], wv[...], ACROSS, preferred_element_type=F32)
+        total = lax.dot_general(heads(gk, k), wk[...], ACROSS, preferred_element_type=F32)
+        total += lax.dot_general(heads(gv, k), wv[...], ACROSS, preferred_element_type=F32)
         for h, (tile, part) in enumerate(UNITS[k]):
             half_total = total[h * HALF:(h + 1) * HALF]
             if tile == 0:
@@ -405,7 +407,7 @@
         rows = slice(a * 2 * TILE, (a + 1) * 2 * TILE)
         side = slice(j * DEPTH, (j + 1) * DEPTH)
         src, dst = ((gk, kgrad), (gv, vgrad))[j]
-        rhs = jnp.concatenate([src[2 * a], src[2 * a + 1]], axis=0)
+        rhs = jnp.concatenate([heads(src, 2 * a), heads(src, 2 * a + 1)], axis=0)
         total = jnp.dot(ft[:, rows], rhs, preferred_element_type=F32)
         if a == 0:
             expo[0:3 * SEQ, side] = total[0:3 * SEQ]
@@ -435,8 +437,8 @@
     two(1)
     three(0)
     one(3)
+    two(2)
     forward()
-    two(2)
     three(1)
     two(3)
     weights(0, 0)
@@ -500,8 +502,8 @@
             vmem((TILE, wide), BF16),
             vmem((4, TILE, HD), BF16),
             vmem((4, TILE, HD), BF16),
-            vmem((4, TILE, GROUP * HD), BF16),
-            vmem((4, TILE, GROUP * HD), BF16),
+            vmem((4, 8, TILE, HD), BF16),
+            vmem((4, 8, TILE, HD), BF16),
             vmem((4, 2, HALF, DEPTH), BF16),
             vmem((4, 2, HALF, DEPTH), BF16),
             vmem((TILE, DEPTH), F32),
@@ -510,7 +512,7 @@
             vmem((1, SEQ), jnp.int32),
             dma((7,)), dma, dma, dma, dma((3, 2)),
             dma((8,)), dma((8,)), dma((6,)), dma((6,)), dma((8,)), dma((8,)),
-            dma((4,)), dma((4,)), dma((4,)), dma((2,)), dma,
+            dma((4,)), dma((4, 2)), dma((4,)), dma((4,)), dma((4,)), dma((2,)), dma,
         ],
         compiler_params=pltpu.CompilerParams(
             collective_id=1, has_side_effects=True, vmem_limit_bytes=VMEM_LIMIT

time: 73.2 us -> 71.7 us (0.980)
  Pallas kernels: 72.3 us -> 70.8 us
    pallas_call x1, Pallas kernels: 70 us -> 68.4 us  [main(): pl.pallas_call(main_kernel, out_shape=(vmem((DEPTH, GROUP * HD), BF16), v...]
where the time goes in v4:
time: 71.7 us; the launch traced here: 71.6 us
  Pallas kernels  70.8 us (99%)
  between operations  0.8 us (1%)
    pallas_call x1, Pallas kernels, main(): pl.pallas_call(main_kernel, out_shape=(vmem((DEPTH, GROUP * HD), BF16), v...  68.4 us
    pallas_call x1, Pallas kernels, close(): pl.pallas_call(close_kernel, out_shape=tuple((jax.ShapeDtypeStruct(x.shap...  2.35 us

profile of v4, /device:TPU:64, one launch (start us, length us, event | category | flops | bytes accessed | tf_op | source)
XLA Modules:
  0.0 71.6 jit_solution(11737635483947371240)
XLA Ops:
  0.6 68.4 %main.1 = (bf16[1024,1024]{1,0:T(8,128)(2,1)S(1)}, bf16[1024,1024]{1,0:T(8,128)(2,1)S(1)}, bf16[256,1024]{1,0:T(8,128)(2,1)S(1)}, bf16[192,1024]{1,0:T(8,128)(2,1)S(1)}) custom-call(s32[4]{0:T(128)} %count_hbm.1, s32[1,256]{1,0:T(1,128)} %bitcast.12, bf16[192,1024]{1,0:T(8,128)(2,1)} %f_ref.1, bf16[1024,1024]{1,0:T(8,128)(2,1)} %bitcast.8, ...), custom_call_target="tpu_custom_call" | custom-call | tf_op jit(solution)/shard_map/main/pallas_call | solution.py:467
  69.1 2.3 %close.1 = (bf16[1024,1024]{1,0:T(8,128)(2,1)}, bf16[1024,1024]{1,0:T(8,128)(2,1)}, bf16[256,1024]{1,0:T(8,128)(2,1)}, bf16[192,1024]{1,0:T(8,128)(2,1)}) custom-call(bf16[1024,1024]{1,0:T(8,128)(2,1)S(1)} %get-tuple-element.12.refs_0_, bf16[1024,1024]{1,0:T(8,128)(2,1)S(1)} %get-tuple-element.13.refs_1_, bf16[256,1024]{1,0:T(8,128)(2,1)S(1)} %get-tuple-element.14.refs_2_, ...), custom_call_target="tpu_custom_call" | custom-call | tf_op jit(solution)/shard_map/close/pallas_call | solution.py:544

commit v5 on v4

--- a/solution.py
+++ b/solution.py
@@ -17,6 +17,7 @@
 RING = 4
 TILE = 192
 HALF = TILE // 2
+PITCH = 256
 DEPTH = 1024
 SEQ = 256
 LEVELS = 32700.0
@@ -262,9 +263,9 @@
             sums[i:i + 1, wide] = jnp.sum(e, axis=0, keepdims=True)
             dots[i:i + 1, wide] = jnp.sum(e * dprob, axis=0, keepdims=True)
 
-    def turn(a):
-        rows = [fg[k, h * HALF:(h + 1) * HALF, :] for k, h in ROWS[4 * a:4 * a + 4]]
-        ft[:, a * 2 * TILE:(a + 1) * 2 * TILE] = jnp.concatenate(rows, axis=0).T
+    def turn(k):
+        rows = [fg[tile, h * HALF:(h + 1) * HALF, :] for tile, h in UNITS[k]]
+        ft[:, k * PITCH:k * PITCH + TILE] = jnp.concatenate(rows, axis=0).T
 
     loads[0].wait()
     loads[1].wait()
@@ -307,14 +308,12 @@
     start(7)
     middle(5)
     relay(4)
+    middle(6)
+    middle(7)
+    relay(5)
     finish(2)
-    middle(6)
-    relay(5)
     finish(3)
-    middle(7)
     finish(4)
-    turn(0)
-    turn(1)
     finish(5)
     finish(6)
     finish(7)
@@ -403,18 +402,20 @@
             else:
                 go(fs.at[tile, part], fr.at[SLOT[SECTIONS - way], part], out3, part_sem, along_x(way))
 
-    def weights(a, j):
-        rows = slice(a * 2 * TILE, (a + 1) * 2 * TILE)
-        side = slice(j * DEPTH, (j + 1) * DEPTH)
-        src, dst = ((gk, kgrad), (gv, vgrad))[j]
-        rhs = jnp.concatenate([heads(src, 2 * a), heads(src, 2 * a + 1)], axis=0)
-        total = jnp.dot(ft[:, rows], rhs, preferred_element_type=F32)
-        if a == 0:
-            expo[0:3 * SEQ, side] = total[0:3 * SEQ]
-            dprobs[0:SEQ, side] = total[3 * SEQ:4 * SEQ]
-        else:
-            dst[0:3 * SEQ, :] = (expo[0:3 * SEQ, side] + total[0:3 * SEQ]).astype(BF16)
-            dst[3 * SEQ:4 * SEQ, :] = (dprobs[0:SEQ, side] + total[3 * SEQ:4 * SEQ]).astype(BF16)
+    def weights(k):
+        for j, (src, dst) in enumerate(((gk, kgrad), (gv, vgrad))):
+            side = slice(j * DEPTH, (j + 1) * DEPTH)
+            total = jnp.dot(ft[:, k * PITCH:k * PITCH + TILE], heads(src, k), preferred_element_type=F32)
+            for held, out in (
+                (expo.at[0:3 * SEQ, side], slice(0, 3 * SEQ)),
+                (dprobs.at[0:SEQ, side], slice(3 * SEQ, 4 * SEQ)),
+            ):
+                if k == 0:
+                    held[...] = total[out]
+                elif k < 3:
+                    held[...] += total[out]
+                else:
+                    dst[out, :] = (held[...] + total[out]).astype(BF16)
 
     def forward():
         turned = values[...].T
@@ -426,27 +427,29 @@
     zero(0)
     attend(1)
     zero(1)
+    for k in range(4):
+        turn(k)
+    attend(2)
     one(0)
-    attend(2)
     zero(2)
+    attend(3)
     one(1)
     two(0)
-    attend(3)
     zero(3)
     one(2)
     two(1)
-    three(0)
     one(3)
     two(2)
+    three(0)
     forward()
+    weights(0)
+    two(3)
     three(1)
-    two(3)
-    weights(0, 0)
     three(2)
-    weights(0, 1)
     three(3)
-    weights(1, 0)
-    weights(1, 1)
+    weights(1)
+    weights(2)
+    weights(3)
     done(fr.at[pl.ds(0, 2)], part_sem)
     for h in range(2):
         rows = slice(h * HALF, (h + 1) * HALF)
@@ -507,7 +510,7 @@
             vmem((4, 2, HALF, DEPTH), BF16),
             vmem((4, 2, HALF, DEPTH), BF16),
             vmem((TILE, DEPTH), F32),
-            vmem((DEPTH, rows), BF16),
+            vmem((DEPTH, 4 * PITCH), BF16),
             pltpu.SMEM((4,), jnp.int32),
             vmem((1, SEQ), jnp.int32),
             dma((7,)), dma, dma, dma, dma((3, 2)),

time: 71.7 us -> 73.6 us (1.026)
  Pallas kernels: 70.8 us -> 72.7 us
    pallas_call x1, Pallas kernels: 68.4 us -> 70.4 us  [main(): pl.pallas_call(main_kernel, out_shape=(vmem((DEPTH, GROUP * HD), BF16), v...]
where the time goes in v5:
time: 73.6 us; the launch traced here: 73.5 us
  Pallas kernels  72.7 us (99%)
  between operations  0.8 us (1%)
    pallas_call x1, Pallas kernels, main(): pl.pallas_call(main_kernel, out_shape=(vmem((DEPTH, GROUP * HD), BF16), v...  70.4 us
    pallas_call x1, Pallas kernels, close(): pl.pallas_call(close_kernel, out_shape=tuple((jax.ShapeDtypeStruct(x.shap...  2.35 us

profile of v5, /device:TPU:64, one launch (start us, length us, event | category | flops | bytes accessed | tf_op | source)
XLA Modules:
  0.0 73.5 jit_solution(1547629511475095091)
XLA Ops:
  0.6 70.4 %main.1 = (bf16[1024,1024]{1,0:T(8,128)(2,1)S(1)}, bf16[1024,1024]{1,0:T(8,128)(2,1)S(1)}, bf16[256,1024]{1,0:T(8,128)(2,1)S(1)}, bf16[192,1024]{1,0:T(8,128)(2,1)S(1)}) custom-call(s32[4]{0:T(128)} %count_hbm.1, s32[1,256]{1,0:T(1,128)} %bitcast.12, bf16[192,1024]{1,0:T(8,128)(2,1)} %f_ref.1, bf16[1024,1024]{1,0:T(8,128)(2,1)} %bitcast.8, ...), custom_call_target="tpu_custom_call" | custom-call | tf_op jit(solution)/shard_map/main/pallas_call | solution.py:470
  71.0 2.3 %close.1 = (bf16[1024,1024]{1,0:T(8,128)(2,1)}, bf16[1024,1024]{1,0:T(8,128)(2,1)}, bf16[256,1024]{1,0:T(8,128)(2,1)}, bf16[192,1024]{1,0:T(8,128)(2,1)}) custom-call(bf16[1024,1024]{1,0:T(8,128)(2,1)S(1)} %get-tuple-element.12.refs_0_, bf16[1024,1024]{1,0:T(8,128)(2,1)S(1)} %get-tuple-element.13.refs_1_, bf16[256,1024]{1,0:T(8,128)(2,1)S(1)} %get-tuple-element.14.refs_2_, ...), custom_call_target="tpu_custom_call" | custom-call | tf_op jit(solution)/shard_map/close/pallas_call | solution.py:547

commit v6 on v5

--- a/solution.py
+++ b/solution.py
@@ -308,12 +308,14 @@
     start(7)
     middle(5)
     relay(4)
+    finish(2)
     middle(6)
+    relay(5)
+    finish(3)
     middle(7)
-    relay(5)
-    finish(2)
-    finish(3)
     finish(4)
+    for k in range(4):
+        turn(k)
     finish(5)
     finish(6)
     finish(7)
@@ -427,20 +429,18 @@
     zero(0)
     attend(1)
     zero(1)
-    for k in range(4):
-        turn(k)
+    one(0)
     attend(2)
-    one(0)
     zero(2)
-    attend(3)
     one(1)
     two(0)
+    attend(3)
     zero(3)
     one(2)
     two(1)
+    three(0)
     one(3)
     two(2)
-    three(0)
     forward()
     weights(0)
     two(3)

time: 73.6 us -> 70.9 us (0.963)
  Pallas kernels: 72.7 us -> 70.1 us
    pallas_call x1, Pallas kernels: 70.4 us -> 67.7 us  [main(): pl.pallas_call(main_kernel, out_shape=(vmem((DEPTH, GROUP * HD), BF16), v...]
where the time goes in v6:
time: 70.9 us
  Pallas kernels  70.1 us (99%)
  between operations  0.8 us (1%)
    pallas_call x1, Pallas kernels, main(): pl.pallas_call(main_kernel, out_shape=(vmem((DEPTH, GROUP * HD), BF16), v...  67.7 us
    pallas_call x1, Pallas kernels, close(): pl.pallas_call(close_kernel, out_shape=tuple((jax.ShapeDtypeStruct(x.shap...  2.35 us

profile of v6, /device:TPU:64, one launch (start us, length us, event | category | flops | bytes accessed | tf_op | source)
XLA Modules:
  0.0 70.9 jit_solution(1788075974394683336)
XLA Ops:
  0.6 67.7 %main.1 = (bf16[1024,1024]{1,0:T(8,128)(2,1)S(1)}, bf16[1024,1024]{1,0:T(8,128)(2,1)S(1)}, bf16[256,1024]{1,0:T(8,128)(2,1)S(1)}, bf16[192,1024]{1,0:T(8,128)(2,1)S(1)}) custom-call(s32[4]{0:T(128)} %count_hbm.1, s32[1,256]{1,0:T(1,128)} %bitcast.12, bf16[192,1024]{1,0:T(8,128)(2,1)} %f_ref.1, bf16[1024,1024]{1,0:T(8,128)(2,1)} %bitcast.8, ...), custom_call_target="tpu_custom_call" | custom-call | tf_op jit(solution)/shard_map/main/pallas_call | solution.py:470
  68.3 2.3 %close.1 = (bf16[1024,1024]{1,0:T(8,128)(2,1)}, bf16[1024,1024]{1,0:T(8,128)(2,1)}, bf16[256,1024]{1,0:T(8,128)(2,1)}, bf16[192,1024]{1,0:T(8,128)(2,1)}) custom-call(bf16[1024,1024]{1,0:T(8,128)(2,1)S(1)} %get-tuple-element.12.refs_0_, bf16[1024,1024]{1,0:T(8,128)(2,1)S(1)} %get-tuple-element.13.refs_1_, bf16[256,1024]{1,0:T(8,128)(2,1)S(1)} %get-tuple-element.14.refs_2_, ...), custom_call_target="tpu_custom_call" | custom-call | tf_op jit(solution)/shard_map/close/pallas_call | solution.py:547
